TPU v7x, 128 devices: a whole 4x4x4 slice. The times are simulated.
128 devices in a mesh: req: 32 (over y, z, core), grp: 4 (over x).
Axes of the slice: x: 4, y: 4, z: 4, core: 2. Of those that a mesh axis runs over, the one named last changes fastest.
Arguments:
- residual_in: bfloat16 [2048, 2048], P('grp'), may hold values from -6 to 6
- mixer_in: bfloat16 [2048, 3, 2048], P('grp', None, 'req'), may hold values from -6 to 6
- forget_floor: float32 [2048], replicated, may hold values from 0.3 to 0.97
- conv_weight: float32 [4, 2048], P(None, 'req'), may hold values from -3 to 3
- conv_edges: bfloat16 [128, 3, 2048], P('grp', None, 'req'), may hold values from -6 to 6
- state_in: float32 [128, 2048, 128], P('grp', 'req'), may hold values from -6 to 6
- accepted: int32 [128], P('grp'), may hold values from 0 to 16
- home_slot: int32 [128], replicated, may hold values from 0 to 127, each once
- gain_mixer: float32 [2048], P('req'), may hold values from 0.1 to 1.9
- w_out: bfloat16 [2048, 2048], P('req'), may hold values from -0.25 to 0.25
- gain_mlp: float32 [2048], replicated, may hold values from 0.1 to 1.9
- w_gate: bfloat16 [2048, 5632], P(None, 'req'), may hold values from -0.125 to 0.125
- w_up: bfloat16 [2048, 5632], P(None, 'req'), may hold values from -0.125 to 0.125
- w_down: bfloat16 [5632, 2048], P('req'), may hold values from -0.15625 to 0.15625
- gain_next: float32 [2048], replicated, may hold values from 0.1 to 1.9
- w_next: bfloat16 [2048, 3, 2048], P(None, None, 'req'), may hold values from -0.125 to 0.125
Outputs:
- next_mixer: bfloat16 [2048, 3, 2048], P('grp', None, 'req')
- kept_state: float32 [128, 2048, 128], P('grp', 'req')
- kept_edges: bfloat16 [128, 3, 2048], P('grp', None, 'req')
Inputs may be any that keep to these rules, and one draw needn't show every extreme that they name: `home_slot`: every row of the kept outputs is the home of exactly one request.
All inputs are finite; a program needn't handle non-finite values.
Results may differ from a plain program's by a relative error of at most 0.029.
Values may be sent and summed in bfloat16 or wider, within the bound.
A program may use at most 64 MiB of HBM per device.

v0:
```python
import jax
import jax.numpy as jnp
from jax import lax
from jax.sharding import PartitionSpec as P

EPSILON = 1e-06


def partner_2(block, axis, apart):
    count = lax.axis_size(axis)
    route = []
    for low in range(count):
        high = low | 1 << apart
        if high != low and high < count:
            route += [(low, high), (high, low)]
    return lax.ppermute(block, axis, route)


def scaled_norm(values_in, gain_row):
    widened = values_in.astype(jnp.float32)
    factor = lax.rsqrt(jnp.mean(widened * widened, axis=1, keepdims=True) + EPSILON)
    return (widened * factor * gain_row).astype(jnp.bfloat16)


def per_device(
    residual_in,
    mixer_in,
    forget_floor,
    conv_weight,
    conv_edges,
    state_in,
    accepted,
    home_slot,
    gain_mixer,
    w_out,
    gain_mlp,
    w_gate,
    w_up,
    w_down,
    gain_next,
    w_next,
):
    token_rows = residual_in.shape[0]
    model_width = residual_in.shape[1]
    local_width = mixer_in.shape[2]
    requests = state_in.shape[0]
    key_width = state_in.shape[2]
    draft_steps = token_rows // requests
    tap_count = conv_weight.shape[0]
    member = lax.axis_index("req")
    own_halves = mixer_in[:, 0:2]
    partner = partner_2(own_halves, "req", 0)
    lower_half = member % 2 == 0
    key_side = jnp.where(
        lower_half,
        jnp.concatenate([own_halves, partner], axis=2),
        jnp.concatenate([partner, own_halves], axis=2),
    )
    head_count = local_width // local_width
    key_start = member * local_width // key_width * key_width
    forget_low = lax.dynamic_slice_in_dim(forget_floor, key_start, head_count * key_width, 0)
    query = jax.nn.silu(key_side[:, 0].astype(jnp.float32))
    forget = forget_low + (1.0 - forget_low) * jax.nn.sigmoid(key_side[:, 1].astype(jnp.float32))
    keyed = 1.0 - forget
    sequence = jnp.concatenate(
        [conv_edges, mixer_in[:, 2].reshape(requests, draft_steps, local_width)], axis=1
    )
    seq_float = sequence.astype(jnp.float32)
    conv_input = sum(
        (
            conv_weight[offset] * seq_float[:, offset : offset + draft_steps]
            for offset in range(tap_count)
        )
    )

    def by_step(array_in, inner_width):
        shaped = array_in.reshape(requests, draft_steps, head_count, inner_width)
        return jnp.moveaxis(shaped, 1, 0)

    step_inputs = (
        by_step(query, key_width),
        by_step(forget, key_width),
        by_step(keyed, key_width),
        by_step(conv_input, local_width),
    )
    head_scale = key_width ** (-0.5)

    def advance(carry, inputs_now):
        current, kept, counter = carry
        q_step, f_step, k_step, v_step = inputs_now
        current = f_step[:, :, None, :] * current + v_step[:, :, :, None] * k_step[:, :, None, :]
        output = jnp.sum(current * q_step[:, :, None, :], axis=3) * head_scale
        kept = jnp.where((counter + 1 == accepted)[:, None, None, None], current, kept)
        return ((current, kept, counter + 1), output)

    begin_state = state_in.reshape(requests, head_count, local_width, key_width)
    carry_out, outputs = lax.scan(advance, (begin_state, begin_state, jnp.int32(0)), step_inputs)
    kept_local = carry_out[1].reshape(requests, local_width, key_width)
    mixed = jnp.moveaxis(outputs, 0, 1).reshape(token_rows, local_width)
    gained = (mixed * gain_mixer).astype(jnp.bfloat16)
    partial_squares = jnp.sum(mixed * mixed, axis=1)
    mixer_terms = jnp.dot(gained, w_out, preferred_element_type=jnp.float32)
    mixer_sum, squares = (
        lax.psum(mixer_terms.astype(jnp.bfloat16), "req").astype(jnp.float32),
        lax.psum(partial_squares.astype(jnp.bfloat16), "req").astype(jnp.float32),
    )
    attn = mixer_sum * lax.rsqrt(squares[:, None] / model_width + EPSILON)
    first = (residual_in.astype(jnp.float32) + attn).astype(jnp.bfloat16)
    normed = scaled_norm(first, gain_mlp)
    gate = jnp.dot(normed, w_gate, preferred_element_type=jnp.float32)
    up_part = jnp.dot(normed, w_up, preferred_element_type=jnp.float32)
    hidden = (jax.nn.silu(gate) * up_part).astype(jnp.bfloat16)
    next_weight = w_next.reshape(model_width, 3 * local_width)
    down_terms = jnp.dot(hidden, w_down, preferred_element_type=jnp.float32)
    down = lax.psum(down_terms.astype(jnp.bfloat16), "req").astype(jnp.float32)
    second = (first.astype(jnp.float32) + down).astype(jnp.bfloat16)
    final_norm = scaled_norm(second, gain_next)
    next_flat = jnp.dot(final_norm, next_weight, preferred_element_type=jnp.float32)
    next_mixer = next_flat.astype(jnp.bfloat16).reshape(token_rows, 3, local_width)
    edge_count = conv_edges.shape[1]
    edge_index = accepted[:, None] + jnp.arange(edge_count, dtype=jnp.int32)[None, :]
    kept_edge = jnp.take_along_axis(sequence, edge_index[:, :, None], axis=1)
    group_start = lax.axis_index("grp") * requests
    empty_state = jnp.zeros_like(kept_local)
    empty_edges = jnp.zeros(kept_edge.shape, jnp.float32)
    state_acc = empty_state
    edge_acc = empty_edges
    state_piece = lax.all_gather(kept_local.astype(jnp.bfloat16), "grp", axis=0, tiled=True).astype(
        jnp.float32
    )
    edge_piece = lax.all_gather(
        kept_edge.astype(jnp.float32).astype(jnp.bfloat16), "grp", axis=0, tiled=True
    ).astype(jnp.float32)
    target = home_slot - group_start
    inside = (target >= 0) & (target < requests)
    target = jnp.where(inside, target, requests)
    state_acc = state_acc.at[target].set(state_piece, mode="drop")
    edge_acc = edge_acc.at[target].set(edge_piece, mode="drop")
    return (next_mixer, state_acc, edge_acc.astype(jnp.bfloat16))


def solution(mesh):
    in_specs = (
        P("grp", None),
        P("grp", None, "req"),
        P(),
        P(None, "req"),
        P("grp", None, "req"),
        P("grp", "req", None),
        P("grp"),
        P(),
        P("req"),
        P("req", None),
        P(),
        P(None, "req"),
        P(None, "req"),
        P("req", None),
        P(),
        P(None, None, "req"),
    )
    out_specs = (P("grp", None, "req"), P("grp", "req", None), P("grp", None, "req"))
    return jax.shard_map(
        per_device, mesh=mesh, in_specs=in_specs, out_specs=out_specs, check_vma=False
    )
```

profile of v0, /device:TPU:1, one launch (start us, length us, event | category | flops | bytes accessed | tf_op | source)
XLA Modules:
  0.0 312.3 jit_solution(15410177543315030601)
XLA Ops:
  8.1 1.3 copy.83
  10.5 1.5 collective-permute-start
  17.4 35.0 %while.17 = (s32[]{:T(128)}, f32[32,1,64,128]{3,2,1,0:T(8,128)S(1)}, bf16[32,1,64,128]{3,2,1,0:T(8,128)(2,1)S(1)}, f32[16,32,1,64]{3,2,1,0:T(1,128)S(1)}, f32[16...) while((s32[]{:T(128)}, ...), condition=%wide.region_2.3_spmd, body=%wide.region_0.2_spmd.sunk | while | flops 1572898 | bytes 4424001 | solution.py:97
  17.4 0.9 constant_dynamic-slice_fusion.5
  19.6 0.9 constant_dynamic-slice_fusion.5
  21.8 0.9 constant_dynamic-slice_fusion.5
  24.0 0.9 constant_dynamic-slice_fusion.5
  26.2 0.9 constant_dynamic-slice_fusion.5
  34.9 0.9 constant_dynamic-slice_fusion.5
  37.1 0.9 constant_dynamic-slice_fusion.5
  39.3 0.9 constant_dynamic-slice_fusion.5
  41.5 0.9 constant_dynamic-slice_fusion.5
  43.7 0.9 constant_dynamic-slice_fusion.5
  45.9 0.9 constant_dynamic-slice_fusion.5
  48.0 0.9 constant_dynamic-slice_fusion.5
  50.2 0.9 constant_dynamic-slice_fusion.5
  52.6 2.9 convolution_convert_fusion.1
  55.6 1.1 multiply_reduce_fusion.1
  57.0 63.9 %psum.22 = bf16[512]{0:T(512)(128)(2,1)S(1)} all-reduce(bf16[512]{0:T(512)(128)(2,1)S(1)} %convert_element_type.109), channel_id=1, replica_groups=mesh['req'=32,'grp'=4] {'req'}, use_global_device_ids=true, to_apply=%region_5.6 | all-reduce | flops 512 | bytes 2048 | tf_op jit(solution)/shard_map/psum | solution.py:105
  120.9 44.4 %all-reduce.3.cloned.1.call-done = bf16[512,2048]{1,0:T(8,128)(2,1)} async-done(((bf16[512,2048]{1,0:T(8,128)(2,1)}), bf16[512,2048]{1,0:T(8,128)(2,1)}) %all-reduce.3.cloned.1.call-update) | async-done | bytes 2097168 | tf_op jit(solution)/shard_map/psum | solution.py:104
  165.3 3.2 %fusion.3 = (f32[512]{0:T(512)S(1)}, bf16[512,2048]{1,0:T(8,128)(2,1)S(1)}) fusion(f32[512]{0:T(512)S(1)} %add_rsqrt_fusion.2, bf16[512,2048]{1,0:T(8,128)(2,1)} %all-reduce.3.cloned.1.call-done, bf16[512,2048]{1,0:T(8,128)(2,1)} %param.18), kind=kLoop, calls=%fused_computation.21 | loop fusion | flops 8388096 | bytes 6295552 | tf_op jit(solution)/shard_map/reduce_sum | solution.py:21
  168.5 2.0 fusion.18
  170.6 4.3 %convolution_convert_fusion = bf16[512,2048]{1,0:T(8,128)(2,1)} fusion(bf16[176,2048]{1,0:T(8,128)(2,1)} %param.31, bf16[2048,176]{0,1:T(8,128)(2,1)} %param.30, bf16[512,2048]{1,0:T(8,128)(2,1)S(1)} %get-tuple-element.226, f32[2048]{0:T(1024)S(1)} %copy-done.8, f32[512]{0:T(512)S(1)} %add_rsqrt_fusion.1, f32[512,176]{0,1:T(8,128)S(1)} %fusion.18), kind=kOutput, calls=%fused_computation.26 | convolution fusion | flops 743981056 | bytes 6006784 | tf_op jit(solution)/shard_map/dot_general | solution.py:114
  175.6 1.5 gather_fusion
  177.4 9.7 %all_gather.7 = bf16[128,3,64]{2,0,1:T(8,128)(2,1)S(1)} all-gather(bf16[32,3,64]{2,0,1:T(8,128)(2,1)S(1)} %copy.53), channel_id=1, replica_groups=mesh['req'=32,'grp'=4] {'grp'}, dimensions={0}, use_global_device_ids=true | all-gather | bytes 61440 | tf_op jit(solution)/shard_map/all_gather | solution.py:131
  187.4 4.6 %scatter_fusion.1 = f32[32,3,64]{2,1,0:T(4,128)S(1)} fusion(f32[32,3,64]{2,1,0:T(4,128)S(1)} %broadcast_in_dim.72, s32[128]{0:T(128)S(1)} %compare_select_fusion.2, f32[128,3,64]{2,1,0:T(4,128)S(1)} %copy.55), kind=kCustom, calls=%fused_computation.2 | custom fusion | bytes 295424 | tf_op jit(solution)/shard_map/scatter | solution.py:138
  192.7 90.1 %all-reduce.5.cloned.1.call-done = bf16[512,2048]{1,0:T(8,128)(2,1)} async-done(((bf16[512,2048]{1,0:T(8,128)(2,1)}), bf16[512,2048]{1,0:T(8,128)(2,1)}) %all-reduce.5.cloned.1.call-update) | async-done | bytes 2097168 | tf_op jit(solution)/shard_map/psum | solution.py:115
  282.7 2.5 fusion
  285.3 1.8 fusion.11
  287.0 4.0 %bitcast_convert_fusion = f32[128,64,128]{2,1,0:T(8,128)} fusion(bf16[128,1,64,128]{3,2,1,0:T(8,128)(2,1)} %all-gather.3.cloned.1.call-done), kind=kLoop, calls=%fused_computation.29 | loop fusion | flops 1048576 | bytes 6291456 | tf_op jit(solution)/shard_map/convert_element_type | solution.py:128
  291.1 12.8 %scatter_fusion = f32[32,64,128]{2,1,0:T(8,128)S(1)} fusion(f32[32,64,128]{2,1,0:T(8,128)S(1)} %broadcast_in_dim.70, s32[128]{0:T(128)S(1)} %compare_select_fusion.2, f32[128,64,128]{2,1,0:T(8,128)} %bitcast_convert_fusion), kind=kCustom, calls=%fused_computation.1 | custom fusion | bytes 12583424 | tf_op jit(solution)/shard_map/scatter | solution.py:137
  303.9 1.0 copy-done.1
  (181 shorter events, 30.7 us)
Async XLA Ops:
  8.0 277.2 %copy-start = (bf16[2048,3,64]{0,2,1:T(8,128)(2,1)S(1)}, bf16[2048,3,64]{0,2,1:T(8,128)(2,1)}, u32[]{:S(2)}) copy-start(bf16[2048,3,64]{0,2,1:T(8,128)(2,1)} %param.33) | copy-start | bytes 2359300
  8.0 157.3 %all-reduce.3.cloned.1.call-start = ((), (), s32[]{:S(2)}) async-start(), calls=%async_computation | async-start | bytes 4194304 | tf_op jit(solution)/shard_map/psum | solution.py:104
  9.3 8.1 %copy-start.7 = (s32[32]{0:T(128)S(1)}, s32[32]{0:T(128)}, u32[]{:S(2)}) copy-start(s32[32]{0:T(128)} %param.24) | copy-start | bytes 388
  10.5 5.8 %collective-permute-start = (bf16[512,2,64]{2,0,1:T(8,128)(2,1)S(1)}, bf16[512,2,64]{2,0,1:T(8,128)(2,1)S(1)}, u32[]{:S(2)}, u32[]{:S(2)}) collective-permute-start(bf16[512,2,64]{2,0,1:T(8,128)(2,1)S(1)} %copy.60), channel_id=1, source_target_pairs={{0,4},{4,0},{8,12},{12,8},{16,20},{20,16},{24,28},{28,24},{32,36},... | collective-permute-start | bytes 393224 | tf_op jit(solution)/shard_map/ppermute | solution.py:16
  14.5 0.7 copy-start.4
  17.4 35.1 %copy-start.6 = (f32[64]{0:T(128)S(1)}, f32[64]{0:T(128)}, u32[]{:S(2)}) copy-start(f32[64]{0:T(128)} %param.26) | copy-start | bytes 772
  52.4 116.1 %copy-start.2 = (bf16[32,1,64,128]{3,2,1,0:T(8,128)(2,1)}, bf16[32,1,64,128]{3,2,1,0:T(8,128)(2,1)S(1)}, u32[]{:S(2)}) copy-start(bf16[32,1,64,128]{3,2,1,0:T(8,128)(2,1)S(1)} %get-tuple-element.159) | copy-start | bytes 1572868
  55.6 113.0 %copy-start.8 = (f32[2048]{0:T(1024)S(1)}, f32[2048]{0:T(1024)}, u32[]{:S(2)}) copy-start(f32[2048]{0:T(1024)} %param.28) | copy-start | bytes 24580
  55.6 227.1 %all-reduce.5.cloned.1.call-start = ((), (), s32[]{:S(2)}) async-start(), calls=%async_computation.1 | async-start | bytes 4194304 | tf_op jit(solution)/shard_map/psum | solution.py:115
  170.6 5.1 %copy-start.5 = (bf16[32,19,64]{2,0,1:T(8,128)(2,1)S(1)}, bf16[32,19,64]{2,0,1:T(8,128)(2,1)}, u32[]{:S(2)}) copy-start(bf16[32,19,64]{2,0,1:T(8,128)(2,1)} %copy-done.4) | copy-start | bytes 233476
  170.6 16.8 %copy-start.10 = (s32[128]{0:T(128)S(1)}, s32[128]{0:T(128)}, u32[]{:S(2)}) copy-start(s32[128]{0:T(128)} %param.25) | copy-start | bytes 1540
  174.8 110.4 %copy-start.9 = (f32[2048]{0:T(1024)S(1)}, f32[2048]{0:T(1024)}, u32[]{:S(2)}) copy-start(f32[2048]{0:T(1024)} %param.32) | copy-start | bytes 24580
  174.9 112.2 %all-gather.3.cloned.1.call-start = ((), (), s32[]{:S(2)}) async-start(), calls=%async_computation.2 | async-start | bytes 2621440 | tf_op jit(solution)/shard_map/all_gather | solution.py:128
  282.7 2.5 copy-start.3
  303.9 1.0 copy-start.1
Sparse Core Ops, SparseCore 0:
  55.7 109.5 all-reduce.2
  175.0 107.6 all-reduce.4
Sparse Core Ops, SparseCore 1:
  177.6 30.1 all-gather.2
where the time goes:
time: 313 us; the launch traced here: 312 us
  waiting for transfers between devices  135 us (43%)
  blocking collectives  73.7 us (24%)
  local copies, waits for them, and re-layouts  42.7 us (14%)
  other arithmetic  31.4 us (10%)
  between operations  15.9 us (5%)
  matrix products  11 us (4%)
    psum x1, waiting for transfers between devices, per_device(): down = lax.psum(down_terms.astype(jnp.bfloat16), 'req').astype(jnp.float32)  90.1 us
    psum x1, blocking collectives, per_device(): lax.psum(partial_squares.astype(jnp.bfloat16), 'req').astype(jnp.float32)  63.9 us
    psum x1, waiting for transfers between devices, per_device(): lax.psum(mixer_terms.astype(jnp.bfloat16), 'req').astype(jnp.float32)  44.4 us
    dynamic_slice x32, local copies, waits for them, and re-layouts, per_device(): lax.scan(advance, (begin_state, begin_state, jnp.int32(0)), step_inputs)  15.3 us
    reduce_sum x16, other arithmetic, advance(): output = jnp.sum(current * q_step[:, :, None, :], axis=3) * head_scale  14.5 us
    scatter x1, local copies, waits for them, and re-layouts, per_device(): state_acc = state_acc.at[target].set(state_piece, mode='drop')  12.8 us
    all_gather x1, blocking collectives, per_device(): lax.all_gather(kept_edge.astype(jnp.float32).astype(jnp.bfloat16), 'grp',...  9.73 us
  transfers between devices with their start and end apart: 4, of which 2 were waited for; matrix products, arithmetic and copies ran while one was open for 5% of the time, Pallas kernels for 0%

commit v1 on v0

v1 whole, which is shorter than its diff:
```python
import jax
import jax.numpy as jnp
from jax import lax
from jax.experimental import pallas as pl
from jax.experimental.pallas import tpu as pltpu
from jax.sharding import PartitionSpec as P

EPSILON = 1e-06
MESH = pl.DeviceIdType.MESH
F32 = jnp.float32
BF16 = jnp.bfloat16

SIDE = 4
CHIPS = SIDE * SIDE
GROUPS = 4
STEPS = 16
TAPS = 4
EDGES = 3
WIDTH = 2048
HALF = 64
KEYS = 128
EXTRA = 128
REQUESTS = 32
TOKENS = REQUESTS * STEPS
MINE = TOKENS // 2
TILE = 128
TILE_REQ = TILE // STEPS

NT = (((1,), (1,)), ((), ()))
TN = (((0,), (0,)), ((), ()))


def dot(left, right, dims=(((1,), (0,)), ((), ()))):
    return lax.dot_general(left, right, dims, preferred_element_type=F32)


def iota(shape, dim):
    return lax.broadcasted_iota(jnp.int32, shape, dim)


def to_column(row):
    size = row.shape[1]
    square = jnp.broadcast_to(row, (size, size))
    diagonal = iota((size, size), 0) == iota((size, size), 1)
    return jnp.sum(jnp.where(diagonal, square, jnp.zeros_like(square)), axis=1, keepdims=True)


def kernel(
    residual, mixer, floor, taps, edges, state, accepted, home, gain_mixer,
    w_out, gain_mlp, w_gate, w_up, w_down, gain_next, w_next,
    next_out, kept_out, edge_out,
    mix_v, pair, state_v, res_v, wo, wg, wu, wd, wn,
    query_b, key_b, decay, values, picked, gained_own, gained_send, gained_recv,
    send1, recv1, gather1, first_v, hidden, send2, recv2, gather2,
    next_send, next_recv, kept_v, edge_v, kept_all, edge_all,
    load_sem, pair_ss, pair_rs, ss1, rs1, ss2, rs2, ss3, rs3, ss4, rs4, ss_x, rs_x,
):
    member = lax.axis_index("req")
    group = lax.axis_index("grp")
    core = member % 2
    chip = member // 2
    at_y = chip // SIDE
    at_z = chip % SIDE
    sibling = {"req": chip * 2 + (1 - core), "grp": group}

    def peer_chip(k):
        return ((at_y + k // SIDE) % SIDE) * SIDE + (at_z + k % SIDE) % SIDE

    def peer(k):
        return {"req": peer_chip(k) * 2 + core, "grp": group}

    def across(k):
        return {"req": member, "grp": (group + k) % GROUPS}

    barrier = pltpu.get_barrier_semaphore()

    def greet(k, carry):
        pl.semaphore_signal(barrier, inc=1, device_id=peer(k), device_id_type=MESH)
        return carry

    pl.semaphore_signal(barrier, inc=1, device_id=sibling, device_id_type=MESH)
    lax.fori_loop(1, CHIPS, greet, 0)
    for k in range(1, GROUPS):
        pl.semaphore_signal(barrier, inc=1, device_id=across(k), device_id_type=MESH)

    loads = [
        pltpu.make_async_copy(mixer, mix_v, load_sem.at[0]),
        pltpu.make_async_copy(state, state_v, load_sem.at[1]),
        pltpu.make_async_copy(w_out, wo.at[core], load_sem.at[2]),
        pltpu.make_async_copy(
            residual.at[pl.ds(pl.multiple_of(core * MINE + chip * STEPS, STEPS), STEPS)],
            res_v, load_sem.at[3]),
        pltpu.make_async_copy(w_gate, wg.at[core], load_sem.at[4]),
        pltpu.make_async_copy(w_up, wu.at[core], load_sem.at[5]),
        pltpu.make_async_copy(w_down, wd.at[core], load_sem.at[6]),
        pltpu.make_async_copy(w_next, wn.at[core], load_sem.at[7]),
    ]
    for load in loads:
        load.start()

    def to_sibling(source, target, slot):
        return pltpu.make_async_remote_copy(
            src_ref=source, dst_ref=target, send_sem=pair_ss.at[slot], recv_sem=pair_rs.at[slot],
            device_id=sibling, device_id_type=MESH)

    pl.semaphore_wait(barrier, CHIPS + GROUPS - 1)
    halves = to_sibling(mixer.at[0:2], pair.at[:, core], 0)
    halves.start()
    shared = [
        to_sibling(w_out, wo.at[core], 1),
        to_sibling(w_gate, wg.at[core], 2),
        to_sibling(w_up, wu.at[core], 3),
        to_sibling(w_down, wd.at[core], 4),
        to_sibling(w_next, wn.at[core], 5),
    ]
    for copy in shared:
        copy.start()

    loads[0].wait()
    lane = iota((1, TOKENS), 1)
    step_of = lane % STEPS
    inputs_raw = mix_v[2]
    inputs_f = inputs_raw.astype(F32)
    stacked = jnp.concatenate([edges[i] for i in range(EDGES)], axis=0)
    row96 = iota((EDGES * REQUESTS, TOKENS), 0)
    lane96 = iota((EDGES * REQUESTS, TOKENS), 1)
    conv = to_column(taps[TAPS - 1:TAPS, :]) * inputs_f
    for j in range(TAPS - 1):
        shift = TAPS - 1 - j
        early = row96 // REQUESTS - j
        place = (early >= 0) & (lane96 == (row96 % REQUESTS) * STEPS + early)
        from_edges = dot(stacked, jnp.where(place, 1.0, 0.0).astype(BF16), TN)
        moved = jnp.where(step_of >= shift, pltpu.roll(inputs_f, shift, axis=1), 0.0)
        conv = conv + to_column(taps[j:j + 1, :]) * (moved + from_edges)
    values[...] = conv.astype(BF16)

    pair[:, core] = mix_v[0:2]
    floor_row = floor[pl.ds(chip, 1), :]
    low = to_column(floor_row)
    halves.wait()
    for tile in range(TOKENS // TILE):
        at = slice(tile * TILE, (tile + 1) * TILE)
        step_t = iota((KEYS, TILE), 1) % STEPS
        q_pre = pair[0, :, :, at].reshape(KEYS, TILE).astype(F32)
        f_pre = pair[1, :, :, at].reshape(KEYS, TILE).astype(F32)
        query = q_pre * jax.nn.sigmoid(q_pre)
        forget = low + (1.0 - low) * jax.nn.sigmoid(f_pre)
        keyed = 1.0 - forget
        run = forget
        for shift in (1, 2, 4, 8):
            run = jnp.where(step_t >= shift, run * pltpu.roll(run, shift, axis=1), run)
        decay[:, at] = run
        query_b[:, at] = (query * run).astype(BF16)
        key_b[:, at] = (keyed / run).astype(BF16)

    loads[1].wait()
    gain_column = to_column(gain_mixer[...])
    squares = []
    for tile in range(TOKENS // TILE):
        at = slice(tile * TILE, (tile + 1) * TILE)
        q_t = query_b[:, at]
        begin = state_v[tile * TILE_REQ:(tile + 1) * TILE_REQ].astype(BF16).reshape(TILE_REQ * HALF, KEYS)
        through = dot(begin, q_t).reshape(TILE_REQ, HALF, TILE)
        ours = iota((TILE_REQ, HALF, TILE), 0) == iota((TILE_REQ, HALF, TILE), 2) // STEPS
        total = jnp.sum(jnp.where(ours, through, 0.0), axis=0)
        scores = dot(key_b[:, at], q_t, TN)
        source = iota((TILE, TILE), 0)
        sink = iota((TILE, TILE), 1)
        causal = (source // STEPS == sink // STEPS) & (source <= sink)
        scores = jnp.where(causal, scores, 0.0).astype(BF16)
        total = (total + dot(values[:, at], scores)) * KEYS ** (-0.5)
        gained_own[0:HALF, at] = (total * gain_column).astype(BF16)
        square = jnp.sum(total * total, axis=0, keepdims=True)
        gained_own[HALF:HALF + STEPS, at] = jnp.broadcast_to(square, (STEPS, TILE)).astype(BF16)

    own_lanes = pl.ds(pl.multiple_of(core * MINE, MINE), MINE)
    other_lanes = pl.ds(pl.multiple_of((1 - core) * MINE, MINE), MINE)
    gained_send[...] = gained_own[:, other_lanes]
    swap = to_sibling(gained_send, gained_recv, 6)
    swap.start()
    mine = gained_own[:, own_lanes]
    swap.wait()
    theirs = gained_recv[...]
    lower = jnp.where(core == 0, mine[0:HALF], theirs[0:HALF])
    upper = jnp.where(core == 0, theirs[0:HALF], mine[0:HALF])
    both = jnp.concatenate([lower, upper], axis=0)
    loads[2].wait()
    shared[0].wait()
    squares2 = jnp.concatenate([mine[HALF:], theirs[HALF:]], axis=0)
    pick_one = jnp.where(iota((2 * STEPS, EXTRA), 0) % STEPS == 0, 1.0, 0.0).astype(BF16)
    send1[:, :, WIDTH:] = dot(squares2, pick_one, TN).astype(BF16).reshape(CHIPS, STEPS, EXTRA)
    cut = 512

    def project(n, carry):
        at = pl.ds(pl.multiple_of(n * cut, cut), cut)
        block = wo[:, :, at].reshape(2 * HALF, cut)
        send1[:, :, at] = dot(both, block, TN).astype(BF16).reshape(CHIPS, STEPS, cut)
        return carry

    lax.fori_loop(0, WIDTH // cut, project, 0)

    def scatter(source, target, ssem, rsem):
        def copy(k):
            return pltpu.make_async_remote_copy(
                src_ref=source.at[peer_chip(k)], dst_ref=target.at[k], send_sem=ssem.at[k],
                recv_sem=rsem.at[k], device_id=peer(k), device_id_type=MESH)
        return copy

    def gather(source, target, ssem, rsem):
        def copy(k):
            return pltpu.make_async_remote_copy(
                src_ref=source.at[chip], dst_ref=target.at[chip], send_sem=ssem.at[k],
                recv_sem=rsem.at[k], device_id=peer(k), device_id_type=MESH)
        return copy

    def start_all(copy):
        def body(k, carry):
            copy(k).start()
            return carry
        lax.fori_loop(1, CHIPS, body, 0)

    def wait_all(copy):
        def body(k, carry):
            copy(k).wait_recv()
            return carry
        lax.fori_loop(1, CHIPS, body, 0)

    def drain(copy):
        def body(k, carry):
            copy(k).wait_send()
            return carry
        lax.fori_loop(1, CHIPS, body, 0)

    copy1 = scatter(send1, recv1, ss1, rs1)
    start_all(copy1)
    recv1[0] = send1[chip]

    acc_column = to_column(accepted[...])
    row32 = iota((REQUESTS, TOKENS), 0)
    lane32 = iota((REQUESTS, TOKENS), 1)
    acc_lanes = jnp.sum(jnp.where(lane32 // STEPS == row32, acc_column, 0), axis=0, keepdims=True)
    last = jnp.where(lane32 == row32 * STEPS + acc_column - 1, 1.0, 0.0)
    last = jnp.where(acc_column > 0, last, 0.0).astype(BF16)
    run_all = decay[...]
    run_high = run_all.astype(BF16)
    run_low = (run_all - run_high.astype(F32)).astype(BF16)
    run_picked = dot(last, run_high, NT) + dot(last, run_low, NT)
    picked[...] = jnp.where(acc_column == 0, 1.0, run_picked)
    live = step_of < acc_lanes
    for tile in range(TOKENS // TILE):
        at = slice(tile * TILE, (tile + 1) * TILE)
        taken = jnp.where(live[:, at], values[:, at].astype(F32), 0.0)
        spread = jnp.broadcast_to(taken[None], (TILE_REQ, HALF, TILE))
        ours = iota((TILE_REQ, HALF, TILE), 0) == iota((TILE_REQ, HALF, TILE), 2) // STEPS
        spread = jnp.where(ours, spread, 0.0).astype(BF16).reshape(TILE_REQ * HALF, TILE)
        added = dot(spread, key_b[:, at], NT)
        for i in range(TILE_REQ):
            r = tile * TILE_REQ + i
            kept_v[r] = (picked[r:r + 1, :] * (state_v[r] + added[i * HALF:(i + 1) * HALF])).astype(BF16)
    for e in range(EDGES):
        place = jnp.where(lane32 == row32 * STEPS + acc_column + (e - EDGES), 1.0, 0.0)
        place = jnp.where(acc_column + e >= EDGES, place, 0.0).astype(BF16)
        kept_edge = dot(place, inputs_raw, NT)
        for i in range(EDGES):
            kept_edge = kept_edge + jnp.where(acc_column + e == i, edges[i].astype(F32), 0.0)
        edge_v[e] = kept_edge.astype(BF16)

    def cross(k):
        return [
            pltpu.make_async_remote_copy(
                src_ref=source, dst_ref=target.at[group], send_sem=ss_x.at[slot, k],
                recv_sem=rs_x.at[slot, k], device_id=across(k), device_id_type=MESH)
            for slot, (source, target) in enumerate(((kept_v, kept_all), (edge_v, edge_all)))
        ]

    crossing = [copy for k in range(1, GROUPS) for copy in cross(k)]
    for copy in crossing:
        copy.start()
    kept_all[group] = kept_v[...]
    edge_all[group] = edge_v[...]

    for load in loads[3:]:
        load.wait()
    wait_all(copy1)

    def total_of(ref, width):
        def add(k, sums):
            return sums + ref[k, :, 0:width].astype(F32)
        return lax.fori_loop(1, CHIPS, add, ref[0, :, 0:width].astype(F32))

    sums = total_of(recv1, WIDTH + EXTRA)
    attn = sums[:, 0:WIDTH] * lax.rsqrt(sums[:, WIDTH:WIDTH + 1] / WIDTH + EPSILON)
    first = (res_v[...].astype(F32) + attn).astype(BF16)
    first_v[...] = first

    def scaled_norm(rows, gain):
        wide = rows.astype(F32)
        factor = lax.rsqrt(jnp.mean(wide * wide, axis=1, keepdims=True) + EPSILON)
        return (wide * factor * gain).astype(BF16)

    gather1[chip] = scaled_norm(first, gain_mlp[...])
    copy2 = gather(gather1, gather1, ss2, rs2)
    start_all(copy2)
    drain(copy1)
    for copy in shared[1:]:
        copy.wait()
    wait_all(copy2)

    rows = gather1[...].reshape(MINE, WIDTH)
    for side in range(2):
        gate = dot(rows, wg[side], NT)
        up = dot(rows, wu[side], NT)
        hidden[side] = (gate * jax.nn.sigmoid(gate) * up).astype(BF16)

    def lower_part(n, carry):
        at = pl.ds(pl.multiple_of(n * cut, cut), cut)
        terms = dot(hidden[0], wd[0, :, at]) + dot(hidden[1], wd[1, :, at])
        send2[:, :, at] = terms.astype(BF16).reshape(CHIPS, STEPS, cut)
        return carry

    lax.fori_loop(0, WIDTH // cut, lower_part, 0)
    copy3 = scatter(send2, recv2, ss3, rs3)
    start_all(copy3)
    recv2[0] = send2[chip]
    drain(copy2)

    for copy in crossing:
        copy.wait()
    home_row = home[...]
    source_lane = iota((1, GROUPS * REQUESTS), 1)
    for i in range(REQUESTS):
        found = jnp.max(jnp.where(home_row == group * REQUESTS + i, source_lane, 0))
        kept_out[i] = kept_all[found // REQUESTS, found % REQUESTS]
    target_row = iota((REQUESTS, GROUPS * REQUESTS), 0) + group * REQUESTS
    chosen = jnp.where(home_row == target_row, 1.0, 0.0).astype(BF16)
    for e in range(EDGES):
        pool = edge_all[:, e].reshape(GROUPS * REQUESTS, HALF)
        edge_out[e] = dot(chosen, pool).astype(BF16)

    wait_all(copy3)
    second = (first_v[...].astype(F32) + total_of(recv2, WIDTH)).astype(BF16)
    gather2[chip] = scaled_norm(second, gain_next[...])
    copy4 = gather(gather2, gather2, ss4, rs4)
    start_all(copy4)
    drain(copy3)
    wait_all(copy4)

    normed = gather2[...].reshape(MINE, WIDTH)
    theirs_next = dot(wn[1 - core].reshape(3 * HALF, WIDTH), normed, NT)
    next_send[...] = theirs_next.astype(BF16).reshape(3, HALF, MINE)
    last_swap = to_sibling(next_send, next_recv, 7)
    last_swap.start()
    own_next = dot(wn[core].reshape(3 * HALF, WIDTH), normed, NT)
    next_out[:, :, own_lanes] = own_next.astype(BF16).reshape(3, HALF, MINE)
    drain(copy4)
    last_swap.wait()
    next_out[:, :, other_lanes] = next_recv[...]


def per_device(
    residual_in, mixer_in, forget_floor, conv_weight, conv_edges, state_in, accepted, home_slot,
    gain_mixer, w_out, gain_mlp, w_gate, w_up, w_down, gain_next, w_next,
):
    hidden_width = w_gate.shape[1]
    anywhere = pl.BlockSpec(memory_space=pl.ANY)
    vmem = pl.BlockSpec(memory_space=pltpu.VMEM)
    dma = pltpu.SemaphoreType.DMA
    next_flat, kept, kept_edges = pl.pallas_call(
        kernel,
        name="draft_check",
        out_shape=(
            jax.ShapeDtypeStruct((3, HALF, TOKENS), BF16),
            jax.ShapeDtypeStruct((REQUESTS, HALF, KEYS), BF16),
            jax.ShapeDtypeStruct((EDGES, REQUESTS, HALF), BF16),
        ),
        in_specs=[
            anywhere, anywhere, vmem, vmem, vmem, anywhere, vmem, vmem, vmem,
            anywhere, vmem, anywhere, anywhere, anywhere, vmem, anywhere,
        ],
        out_specs=(vmem, vmem, vmem),
        scratch_shapes=[
            pltpu.VMEM((3, HALF, TOKENS), BF16),
            pltpu.VMEM((2, 2, HALF, TOKENS), BF16),
            pltpu.VMEM((REQUESTS, HALF, KEYS), F32),
            pltpu.VMEM((STEPS, WIDTH), BF16),
            pltpu.VMEM((2, HALF, WIDTH), BF16),
            pltpu.VMEM((2, hidden_width, WIDTH), BF16),
            pltpu.VMEM((2, hidden_width, WIDTH), BF16),
            pltpu.VMEM((2, hidden_width, WIDTH), BF16),
            pltpu.VMEM((2, 3, HALF, WIDTH), BF16),
            pltpu.VMEM((KEYS, TOKENS), BF16),
            pltpu.VMEM((KEYS, TOKENS), BF16),
            pltpu.VMEM((KEYS, TOKENS), F32),
            pltpu.VMEM((HALF, TOKENS), BF16),
            pltpu.VMEM((REQUESTS, KEYS), F32),
            pltpu.VMEM((HALF + STEPS, TOKENS), BF16),
            pltpu.VMEM((HALF + STEPS, MINE), BF16),
            pltpu.VMEM((HALF + STEPS, MINE), BF16),
            pltpu.VMEM((CHIPS, STEPS, WIDTH + EXTRA), BF16),
            pltpu.VMEM((CHIPS, STEPS, WIDTH + EXTRA), BF16),
            pltpu.VMEM((CHIPS, STEPS, WIDTH), BF16),
            pltpu.VMEM((STEPS, WIDTH), BF16),
            pltpu.VMEM((2, MINE, hidden_width), BF16),
            pltpu.VMEM((CHIPS, STEPS, WIDTH), BF16),
            pltpu.VMEM((CHIPS, STEPS, WIDTH), BF16),
            pltpu.VMEM((CHIPS, STEPS, WIDTH), BF16),
            pltpu.VMEM((3, HALF, MINE), BF16),
            pltpu.VMEM((3, HALF, MINE), BF16),
            pltpu.VMEM((REQUESTS, HALF, KEYS), BF16),
            pltpu.VMEM((EDGES, REQUESTS, HALF), BF16),
            pltpu.VMEM((GROUPS, REQUESTS, HALF, KEYS), BF16),
            pltpu.VMEM((GROUPS, EDGES, REQUESTS, HALF), BF16),
            dma((8,)), dma((8,)), dma((8,)),
            dma((CHIPS,)), dma((CHIPS,)), dma((CHIPS,)), dma((CHIPS,)),
            dma((CHIPS,)), dma((CHIPS,)), dma((CHIPS,)), dma((CHIPS,)),
            dma((2, GROUPS)), dma((2, GROUPS)),
        ],
        compiler_params=pltpu.CompilerParams(
            collective_id=0, has_side_effects=True, vmem_limit_bytes=56 * 2**20),
    )(
        residual_in,
        mixer_in.transpose(1, 2, 0),
        forget_floor.reshape(-1, KEYS),
        conv_weight,
        conv_edges.transpose(1, 0, 2),
        state_in,
        accepted.reshape(1, -1),
        home_slot.reshape(1, -1),
        gain_mixer.reshape(1, -1),
        w_out,
        gain_mlp.reshape(1, -1),
        w_gate.T,
        w_up.T,
        w_down,
        gain_next.reshape(1, -1),
        w_next.transpose(1, 2, 0),
    )
    return (
        next_flat.transpose(2, 0, 1),
        kept.astype(F32),
        kept_edges.transpose(1, 0, 2),
    )


def solution(mesh):
    in_specs = (
        P("grp", None),
        P("grp", None, "req"),
        P(),
        P(None, "req"),
        P("grp", None, "req"),
        P("grp", "req", None),
        P("grp"),
        P(),
        P("req"),
        P("req", None),
        P(),
        P(None, "req"),
        P(None, "req"),
        P("req", None),
        P(),
        P(None, None, "req"),
    )
    out_specs = (P("grp", None, "req"), P("grp", "req", None), P("grp", None, "req"))
    return jax.shard_map(
        per_device, mesh=mesh, in_specs=in_specs, out_specs=out_specs, check_vma=False
    )
```

time: 313 us -> 89 us (0.28)
  waiting for transfers between devices: 135 us -> 0 us
  Pallas kernels: 0 us -> 82.9 us
  blocking collectives: 73.7 us -> 0 us
  local copies, waits for them, and re-layouts: 42.7 us -> 2.96 us
  other arithmetic: 31.4 us -> 2.13 us
  between operations: 15.9 us -> 0.65 us
  matrix products: 11 us -> 0 us
    psum x2 -> x0, waiting for transfers between devices: 134 us -> none  [the longest x1 90.1 us: per_device(): down = lax.psum(down_terms.astype(jnp.bfloat16), 'req').astype(jnp.float32)]
    pallas_call x0 -> x1, Pallas kernels: none -> 82.9 us  [per_device(): pl.pallas_call(kernel, name='draft_check', out_shape=(jax.ShapeDtypeStruc...]
    psum x1 -> x0, blocking collectives: 63.9 us -> none  [per_device(): lax.psum(partial_squares.astype(jnp.bfloat16), 'req').astype(jnp.float32)]
    reduce_sum x19 -> x0, other arithmetic: 21.4 us -> none  [the longest x16 14.5 us: advance(): output = jnp.sum(current * q_step[:, :, None, :], axis=3) * head_scale]
    scatter x2 -> x0, local copies, waits for them, and re-layouts: 17.4 us -> none  [the longest x1 12.8 us: per_device(): state_acc = state_acc.at[target].set(state_piece, mode='drop')]
    dynamic_slice x32 -> x0, local copies, waits for them, and re-layouts: 15.3 us -> none  [per_device(): lax.scan(advance, (begin_state, begin_state, jnp.int32(0)), step_inputs)]
    dot_general x4 -> x0, matrix products: 11 us -> none  [the longest x1 4.25 us: per_device(): down_terms = jnp.dot(hidden, w_down, preferred_element_type=jnp.float32)]
    all_gather x1 -> x0, blocking collectives: 9.73 us -> none  [per_device(): lax.all_gather(kept_edge.astype(jnp.float32).astype(jnp.bfloat16), 'grp',...]
  transfers between devices with their start and end apart: 4 -> 0, of which waited for: 2 -> 0; matrix products, arithmetic and copies ran while one was open for 5% -> 0% of each run, Pallas kernels for 0% -> 0%
where the time goes in v1:
time: 89 us; the launch traced here: 88.7 us
  Pallas kernels  82.9 us (93%)
  local copies, waits for them, and re-layouts  2.96 us (3%)
  other arithmetic  2.13 us (2%)
    pallas_call x1, Pallas kernels, per_device(): pl.pallas_call(kernel, name='draft_check', out_shape=(jax.ShapeDtypeStruc...  82.9 us
    unnamed x2, local copies, waits for them, and re-layouts  2.96 us
    convert_element_type x1, other arithmetic, per_device(): kept.astype(F32)  2.13 us

profile of v1, /device:TPU:1, one launch (start us, length us, event | category | flops | bytes accessed | tf_op | source)
XLA Modules:
  0.0 88.7 jit_solution(8890110129294645830)
XLA Ops:
  0.6 82.9 %draft_check.1 = (bf16[3,64,512]{2,1,0:T(8,128)(2,1)}, bf16[32,64,128]{2,1,0:T(8,128)(2,1)}, bf16[3,32,64]{2,1,0:T(8,128)(2,1)}) custom-call(bf16[512,2048]{1,0:T(8,128)(2,1)} %residual.1, bf16[3,64,512]{2,1,0:T(8,128)(2,1)} %bitcast.16, f32[16,128]{1,0:T(8,128)} %bitcast.20, f32[4,64]{1,0:T(4,128)} %taps.1, bf16[3,32,64]{2,1,0:T(8,128)(2,1)} %bitcast.18, ...), custom_call_target="tpu_custom_call" | custom-call | tf_op jit(solution)/shard_map/draft_check/pallas_call | solution.py:368
  83.6 2.1 %convert_element_type.3 = f32[32,64,128]{2,1,0:T(8,128)} convert(bf16[32,64,128]{2,1,0:T(8,128)(2,1)} %get-tuple-element.7) | non-fusion elementwise | flops 262144 | bytes 1572864 | tf_op jit(solution)/shard_map/convert_element_type | solution.py:440
  85.7 1.6 %copy.21 = bf16[512,3,64]{0,2,1:T(8,128)(2,1)} copy(bf16[512,3,64]{0,2,1:T(8,128)(2,1)} %bitcast.17) | data formatting | bytes 393216
  87.3 1.3 %copy.22 = bf16[32,3,64]{2,0,1:T(8,128)(2,1)} copy(bf16[32,3,64]{2,0,1:T(8,128)(2,1)} %bitcast.19) | data formatting | bytes 24576

commit v2 on v1

--- a/solution.py
+++ b/solution.py
@@ -25,6 +25,10 @@
 MINE = TOKENS // 2
 TILE = 128
 TILE_REQ = TILE // STEPS
+CHUNKS = 2
+PART = MINE // CHUNKS
+ROWS = PART // CHIPS
+FOLD = WIDTH // 2
 
 NT = (((1,), (1,)), ((), ()))
 TN = (((0,), (0,)), ((), ()))
@@ -49,9 +53,9 @@
     residual, mixer, floor, taps, edges, state, accepted, home, gain_mixer,
     w_out, gain_mlp, w_gate, w_up, w_down, gain_next, w_next,
     next_out, kept_out, edge_out,
-    mix_v, pair, state_v, res_v, wo, wg, wu, wd, wn,
+    mix_v, pair, state_v, res_v, wo, wgu, wd, wn,
     query_b, key_b, decay, values, picked, gained_own, gained_send, gained_recv,
-    send1, recv1, gather1, first_v, hidden, send2, recv2, gather2,
+    send1, recv1, gather1, first_v, send2, recv2, gather2,
     next_send, next_recv, kept_v, edge_v, kept_all, edge_all,
     load_sem, pair_ss, pair_rs, ss1, rs1, ss2, rs2, ss3, rs3, ss4, rs4, ss_x, rs_x,
 ):
@@ -87,14 +91,15 @@
         pltpu.make_async_copy(mixer, mix_v, load_sem.at[0]),
         pltpu.make_async_copy(state, state_v, load_sem.at[1]),
         pltpu.make_async_copy(w_out, wo.at[core], load_sem.at[2]),
-        pltpu.make_async_copy(
-            residual.at[pl.ds(pl.multiple_of(core * MINE + chip * STEPS, STEPS), STEPS)],
-            res_v, load_sem.at[3]),
-        pltpu.make_async_copy(w_gate, wg.at[core], load_sem.at[4]),
-        pltpu.make_async_copy(w_up, wu.at[core], load_sem.at[5]),
+        pltpu.make_async_copy(w_gate, wgu.at[0, core], load_sem.at[4]),
+        pltpu.make_async_copy(w_up, wgu.at[1, core], load_sem.at[5]),
         pltpu.make_async_copy(w_down, wd.at[core], load_sem.at[6]),
         pltpu.make_async_copy(w_next, wn.at[core], load_sem.at[7]),
     ]
+    for c in range(CHUNKS):
+        near = core * MINE + c * PART + chip // 2 * (2 * ROWS)
+        loads.append(pltpu.make_async_copy(
+            residual.at[pl.ds(pl.multiple_of(near, 2 * ROWS), 2 * ROWS)], res_v.at[c], load_sem.at[8 + c]))
     for load in loads:
         load.start()
 
@@ -108,8 +113,8 @@
     halves.start()
     shared = [
         to_sibling(w_out, wo.at[core], 1),
-        to_sibling(w_gate, wg.at[core], 2),
-        to_sibling(w_up, wu.at[core], 3),
+        to_sibling(w_gate, wgu.at[0, core], 2),
+        to_sibling(w_up, wgu.at[1, core], 3),
         to_sibling(w_down, wd.at[core], 4),
         to_sibling(w_next, wn.at[core], 5),
     ]
@@ -188,29 +193,26 @@
     shared[0].wait()
     squares2 = jnp.concatenate([mine[HALF:], theirs[HALF:]], axis=0)
     pick_one = jnp.where(iota((2 * STEPS, EXTRA), 0) % STEPS == 0, 1.0, 0.0).astype(BF16)
-    send1[:, :, WIDTH:] = dot(squares2, pick_one, TN).astype(BF16).reshape(CHIPS, STEPS, EXTRA)
     cut = 512
 
-    def project(n, carry):
-        at = pl.ds(pl.multiple_of(n * cut, cut), cut)
-        block = wo[:, :, at].reshape(2 * HALF, cut)
-        send1[:, :, at] = dot(both, block, TN).astype(BF16).reshape(CHIPS, STEPS, cut)
-        return carry
-
-    lax.fori_loop(0, WIDTH // cut, project, 0)
-
-    def scatter(source, target, ssem, rsem):
+    def folded(low_part, high_part):
+        width = low_part.shape[1]
+        return jnp.concatenate(
+            [low_part.reshape(CHIPS, ROWS, width), high_part.reshape(CHIPS, ROWS, width)], axis=1
+        ).astype(BF16)
+
+    def scatter(source, target, ssem, rsem, c):
         def copy(k):
             return pltpu.make_async_remote_copy(
-                src_ref=source.at[peer_chip(k)], dst_ref=target.at[k], send_sem=ssem.at[k],
-                recv_sem=rsem.at[k], device_id=peer(k), device_id_type=MESH)
+                src_ref=source.at[c, peer_chip(k)], dst_ref=target.at[c, k], send_sem=ssem.at[c, k],
+                recv_sem=rsem.at[c, k], device_id=peer(k), device_id_type=MESH)
         return copy
 
-    def gather(source, target, ssem, rsem):
+    def gather(target, ssem, rsem, c):
         def copy(k):
             return pltpu.make_async_remote_copy(
-                src_ref=source.at[chip], dst_ref=target.at[chip], send_sem=ssem.at[k],
-                recv_sem=rsem.at[k], device_id=peer(k), device_id_type=MESH)
+                src_ref=target.at[c, chip], dst_ref=target.at[c, chip], send_sem=ssem.at[c, k],
+                recv_sem=rsem.at[c, k], device_id=peer(k), device_id_type=MESH)
         return copy
 
     def start_all(copy):
@@ -231,9 +233,28 @@
             return carry
         lax.fori_loop(1, CHIPS, body, 0)
 
-    copy1 = scatter(send1, recv1, ss1, rs1)
-    start_all(copy1)
-    recv1[0] = send1[chip]
+    copy1 = [scatter(send1, recv1, ss1, rs1, c) for c in range(CHUNKS)]
+    copy2 = [gather(gather1, ss2, rs2, c) for c in range(CHUNKS)]
+    copy3 = [scatter(send2, recv2, ss3, rs3, c) for c in range(CHUNKS)]
+    copy4 = [gather(gather2, ss4, rs4, c) for c in range(CHUNKS)]
+
+    for c in range(CHUNKS):
+        part = slice(c * PART, (c + 1) * PART)
+        square = dot(squares2[:, part], pick_one, TN)
+        send1[c, :, :, FOLD:] = folded(square, square)
+        channels = both[:, part]
+
+        def project(n, carry):
+            at = pl.ds(pl.multiple_of(n * cut, cut), cut)
+            above = pl.ds(pl.multiple_of(FOLD + n * cut, cut), cut)
+            send1[c, :, :, at] = folded(
+                dot(channels, wo[:, :, at].reshape(2 * HALF, cut), TN),
+                dot(channels, wo[:, :, above].reshape(2 * HALF, cut), TN))
+            return carry
+
+        lax.fori_loop(0, FOLD // cut, project, 0)
+        start_all(copy1[c])
+        recv1[c, 0] = send1[c, chip]
 
     acc_column = to_column(accepted[...])
     row32 = iota((REQUESTS, TOKENS), 0)
@@ -279,50 +300,65 @@
     kept_all[group] = kept_v[...]
     edge_all[group] = edge_v[...]
 
+    def total_of(ref, c):
+        def add(k, sums):
+            return sums + ref[c, k].astype(F32)
+        return lax.fori_loop(1, CHIPS, add, ref[c, 0].astype(F32))
+
+    def unfold(block):
+        return jnp.concatenate([block[0:ROWS], block[ROWS:]], axis=1)
+
+    def fold(rows):
+        return jnp.concatenate([rows[:, 0:FOLD], rows[:, FOLD:]], axis=0)
+
+    def scaled_norm(rows, gain):
+        factor = lax.rsqrt(jnp.mean(rows * rows, axis=1, keepdims=True) + EPSILON)
+        return rows * factor * gain
+
+    def all_rows(ref, c):
+        blocks = ref[c].astype(F32)
+        low_part = blocks[:, 0:ROWS].reshape(PART, FOLD)
+        high_part = blocks[:, ROWS:].reshape(PART, FOLD)
+        return jnp.concatenate([low_part, high_part], axis=1).astype(BF16)
+
     for load in loads[3:]:
         load.wait()
-    wait_all(copy1)
-
-    def total_of(ref, width):
-        def add(k, sums):
-            return sums + ref[k, :, 0:width].astype(F32)
-        return lax.fori_loop(1, CHIPS, add, ref[0, :, 0:width].astype(F32))
-
-    sums = total_of(recv1, WIDTH + EXTRA)
-    attn = sums[:, 0:WIDTH] * lax.rsqrt(sums[:, WIDTH:WIDTH + 1] / WIDTH + EPSILON)
-    first = (res_v[...].astype(F32) + attn).astype(BF16)
-    first_v[...] = first
-
-    def scaled_norm(rows, gain):
-        wide = rows.astype(F32)
-        factor = lax.rsqrt(jnp.mean(wide * wide, axis=1, keepdims=True) + EPSILON)
-        return (wide * factor * gain).astype(BF16)
-
-    gather1[chip] = scaled_norm(first, gain_mlp[...])
-    copy2 = gather(gather1, gather1, ss2, rs2)
-    start_all(copy2)
-    drain(copy1)
+    for c in range(CHUNKS):
+        wait_all(copy1[c])
+        sums = total_of(recv1, c)
+        near = res_v[c].astype(F32)
+        before = jnp.where(chip % 2 == 0, near[0:ROWS], near[ROWS:])
+        square = sums[0:ROWS, FOLD:FOLD + 1]
+        attn = unfold(sums[:, 0:FOLD]) * lax.rsqrt(square / WIDTH + EPSILON)
+        first = (before + attn).astype(BF16).astype(F32)
+        first_v[c] = first
+        gather1[c, chip] = fold(scaled_norm(first, gain_mlp[...])).astype(BF16)
+        start_all(copy2[c])
+    for c in range(CHUNKS):
+        drain(copy1[c])
     for copy in shared[1:]:
         copy.wait()
-    wait_all(copy2)
-
-    rows = gather1[...].reshape(MINE, WIDTH)
-    for side in range(2):
-        gate = dot(rows, wg[side], NT)
-        up = dot(rows, wu[side], NT)
-        hidden[side] = (gate * jax.nn.sigmoid(gate) * up).astype(BF16)
-
-    def lower_part(n, carry):
-        at = pl.ds(pl.multiple_of(n * cut, cut), cut)
-        terms = dot(hidden[0], wd[0, :, at]) + dot(hidden[1], wd[1, :, at])
-        send2[:, :, at] = terms.astype(BF16).reshape(CHIPS, STEPS, cut)
-        return carry
-
-    lax.fori_loop(0, WIDTH // cut, lower_part, 0)
-    copy3 = scatter(send2, recv2, ss3, rs3)
-    start_all(copy3)
-    recv2[0] = send2[chip]
-    drain(copy2)
+
+    hidden_width = wd.shape[0] * wd.shape[1]
+    for c in range(CHUNKS):
+        wait_all(copy2[c])
+        both_parts = dot(wgu[...].reshape(2 * hidden_width, WIDTH), all_rows(gather1, c), NT)
+        gate = both_parts[0:hidden_width]
+        hidden = (gate * jax.nn.sigmoid(gate) * both_parts[hidden_width:]).astype(BF16)
+
+        def lower_part(n, carry):
+            at = pl.ds(pl.multiple_of(n * cut, cut), cut)
+            above = pl.ds(pl.multiple_of(FOLD + n * cut, cut), cut)
+            send2[c, :, :, at] = folded(
+                dot(hidden, wd[:, :, at].reshape(hidden_width, cut), TN),
+                dot(hidden, wd[:, :, above].reshape(hidden_width, cut), TN))
+            return carry
+
+        lax.fori_loop(0, FOLD // cut, lower_part, 0)
+        start_all(copy3[c])
+        recv2[c, 0] = send2[c, chip]
+    for c in range(CHUNKS):
+        drain(copy2[c])
 
     for copy in crossing:
         copy.wait()
@@ -337,24 +373,30 @@
         pool = edge_all[:, e].reshape(GROUPS * REQUESTS, HALF)
         edge_out[e] = dot(chosen, pool).astype(BF16)
 
-    wait_all(copy3)
-    second = (first_v[...].astype(F32) + total_of(recv2, WIDTH)).astype(BF16)
-    gather2[chip] = scaled_norm(second, gain_next[...])
-    copy4 = gather(gather2, gather2, ss4, rs4)
-    start_all(copy4)
-    drain(copy3)
-    wait_all(copy4)
-
-    normed = gather2[...].reshape(MINE, WIDTH)
-    theirs_next = dot(wn[1 - core].reshape(3 * HALF, WIDTH), normed, NT)
-    next_send[...] = theirs_next.astype(BF16).reshape(3, HALF, MINE)
-    last_swap = to_sibling(next_send, next_recv, 7)
-    last_swap.start()
-    own_next = dot(wn[core].reshape(3 * HALF, WIDTH), normed, NT)
-    next_out[:, :, own_lanes] = own_next.astype(BF16).reshape(3, HALF, MINE)
-    drain(copy4)
-    last_swap.wait()
-    next_out[:, :, other_lanes] = next_recv[...]
+    for c in range(CHUNKS):
+        wait_all(copy3[c])
+        second = (first_v[c] + unfold(total_of(recv2, c))).astype(BF16).astype(F32)
+        gather2[c, chip] = fold(scaled_norm(second, gain_next[...])).astype(BF16)
+        start_all(copy4[c])
+    for c in range(CHUNKS):
+        drain(copy3[c])
+
+    swaps = []
+    for c in range(CHUNKS):
+        wait_all(copy4[c])
+        normed = all_rows(gather2, c)
+        theirs_next = dot(wn[1 - core].reshape(3 * HALF, WIDTH), normed, NT)
+        next_send[c] = theirs_next.astype(BF16).reshape(3, HALF, PART)
+        swaps.append(to_sibling(next_send.at[c], next_recv.at[c], 7 + c))
+        swaps[c].start()
+        own_next = dot(wn[core].reshape(3 * HALF, WIDTH), normed, NT)
+        here = pl.ds(pl.multiple_of(core * MINE + c * PART, PART), PART)
+        next_out[:, :, here] = own_next.astype(BF16).reshape(3, HALF, PART)
+    for c in range(CHUNKS):
+        drain(copy4[c])
+        swaps[c].wait()
+        there = pl.ds(pl.multiple_of((1 - core) * MINE + c * PART, PART), PART)
+        next_out[:, :, there] = next_recv[c]
 
 
 def per_device(
@@ -382,10 +424,9 @@
             pltpu.VMEM((3, HALF, TOKENS), BF16),
             pltpu.VMEM((2, 2, HALF, TOKENS), BF16),
             pltpu.VMEM((REQUESTS, HALF, KEYS), F32),
-            pltpu.VMEM((STEPS, WIDTH), BF16),
+            pltpu.VMEM((CHUNKS, 2 * ROWS, WIDTH), BF16),
             pltpu.VMEM((2, HALF, WIDTH), BF16),
-            pltpu.VMEM((2, hidden_width, WIDTH), BF16),
-            pltpu.VMEM((2, hidden_width, WIDTH), BF16),
+            pltpu.VMEM((2, 2, hidden_width, WIDTH), BF16),
             pltpu.VMEM((2, hidden_width, WIDTH), BF16),
             pltpu.VMEM((2, 3, HALF, WIDTH), BF16),
             pltpu.VMEM((KEYS, TOKENS), BF16),
@@ -396,23 +437,21 @@
             pltpu.VMEM((HALF + STEPS, TOKENS), BF16),
             pltpu.VMEM((HALF + STEPS, MINE), BF16),
             pltpu.VMEM((HALF + STEPS, MINE), BF16),
-            pltpu.VMEM((CHIPS, STEPS, WIDTH + EXTRA), BF16),
-            pltpu.VMEM((CHIPS, STEPS, WIDTH + EXTRA), BF16),
-            pltpu.VMEM((CHIPS, STEPS, WIDTH), BF16),
-            pltpu.VMEM((STEPS, WIDTH), BF16),
-            pltpu.VMEM((2, MINE, hidden_width), BF16),
-            pltpu.VMEM((CHIPS, STEPS, WIDTH), BF16),
-            pltpu.VMEM((CHIPS, STEPS, WIDTH), BF16),
-            pltpu.VMEM((CHIPS, STEPS, WIDTH), BF16),
-            pltpu.VMEM((3, HALF, MINE), BF16),
-            pltpu.VMEM((3, HALF, MINE), BF16),
+            pltpu.VMEM((CHUNKS, CHIPS, 2 * ROWS, FOLD + EXTRA), BF16),
+            pltpu.VMEM((CHUNKS, CHIPS, 2 * ROWS, FOLD + EXTRA), BF16),
+            pltpu.VMEM((CHUNKS, CHIPS, 2 * ROWS, FOLD), BF16),
+            pltpu.VMEM((CHUNKS, ROWS, WIDTH), F32),
+            pltpu.VMEM((CHUNKS, CHIPS, 2 * ROWS, FOLD), BF16),
+            pltpu.VMEM((CHUNKS, CHIPS, 2 * ROWS, FOLD), BF16),
+            pltpu.VMEM((CHUNKS, CHIPS, 2 * ROWS, FOLD), BF16),
+            pltpu.VMEM((CHUNKS, 3, HALF, PART), BF16),
+            pltpu.VMEM((CHUNKS, 3, HALF, PART), BF16),
             pltpu.VMEM((REQUESTS, HALF, KEYS), BF16),
             pltpu.VMEM((EDGES, REQUESTS, HALF), BF16),
             pltpu.VMEM((GROUPS, REQUESTS, HALF, KEYS), BF16),
             pltpu.VMEM((GROUPS, EDGES, REQUESTS, HALF), BF16),
-            dma((8,)), dma((8,)), dma((8,)),
-            dma((CHIPS,)), dma((CHIPS,)), dma((CHIPS,)), dma((CHIPS,)),
-            dma((CHIPS,)), dma((CHIPS,)), dma((CHIPS,)), dma((CHIPS,)),
+            dma((8 + CHUNKS,)), dma((7 + CHUNKS,)), dma((7 + CHUNKS,)),
+            *[dma((CHUNKS, CHIPS))] * 8,
             dma((2, GROUPS)), dma((2, GROUPS)),
         ],
         compiler_params=pltpu.CompilerParams(

time: 89 us -> 75.2 us (0.84)
  Pallas kernels: 82.9 us -> 69.1 us
    pallas_call x1, Pallas kernels: 82.9 us -> 69.1 us  [per_device(): pl.pallas_call(kernel, name='draft_check', out_shape=(jax.ShapeDtypeStruc...]
where the time goes in v2:
time: 75.2 us; the launch traced here: 74.9 us
  Pallas kernels  69.1 us (92%)
  local copies, waits for them, and re-layouts  2.96 us (4%)
  other arithmetic  2.13 us (3%)
    pallas_call x1, Pallas kernels, per_device(): pl.pallas_call(kernel, name='draft_check', out_shape=(jax.ShapeDtypeStruc...  69.1 us
    unnamed x2, local copies, waits for them, and re-layouts  2.96 us
    convert_element_type x1, other arithmetic, per_device(): kept.astype(F32)  2.13 us

profile of v2, /device:TPU:1, one launch (start us, length us, event | category | flops | bytes accessed | tf_op | source)
XLA Modules:
  0.0 74.9 jit_solution(266610439775777946)
XLA Ops:
  0.6 69.1 %draft_check.1 = (bf16[3,64,512]{2,1,0:T(8,128)(2,1)}, bf16[32,64,128]{2,1,0:T(8,128)(2,1)}, bf16[3,32,64]{2,1,0:T(8,128)(2,1)}) custom-call(bf16[512,2048]{1,0:T(8,128)(2,1)} %residual.1, bf16[3,64,512]{2,1,0:T(8,128)(2,1)} %bitcast.16, f32[16,128]{1,0:T(8,128)} %bitcast.20, f32[4,64]{1,0:T(4,128)} %taps.1, bf16[3,32,64]{2,1,0:T(8,128)(2,1)} %bitcast.18, ...), custom_call_target="tpu_custom_call" | custom-call | tf_op jit(solution)/shard_map/draft_check/pallas_call | solution.py:410
  69.8 2.1 %convert_element_type.3 = f32[32,64,128]{2,1,0:T(8,128)} convert(bf16[32,64,128]{2,1,0:T(8,128)(2,1)} %get-tuple-element.7) | non-fusion elementwise | flops 262144 | bytes 1572864 | tf_op jit(solution)/shard_map/convert_element_type | solution.py:479
  71.9 1.6 %copy.21 = bf16[512,3,64]{0,2,1:T(8,128)(2,1)} copy(bf16[512,3,64]{0,2,1:T(8,128)(2,1)} %bitcast.17) | data formatting | bytes 393216
  73.5 1.3 %copy.22 = bf16[32,3,64]{2,0,1:T(8,128)(2,1)} copy(bf16[32,3,64]{2,0,1:T(8,128)(2,1)} %bitcast.19) | data formatting | bytes 24576

commit v3 on v2

--- a/solution.py
+++ b/solution.py
@@ -29,6 +29,7 @@
 PART = MINE // CHUNKS
 ROWS = PART // CHIPS
 FOLD = WIDTH // 2
+LANES = FOLD // 2
 
 NT = (((1,), (1,)), ((), ()))
 TN = (((0,), (0,)), ((), ()))
@@ -55,7 +56,8 @@
     next_out, kept_out, edge_out,
     mix_v, pair, state_v, res_v, wo, wgu, wd, wn,
     query_b, key_b, decay, values, picked, gained_own, gained_send, gained_recv,
-    send1, recv1, gather1, first_v, send2, recv2, gather2,
+    send1a, send1b, early1a, early1b, middle1a, middle1b, late1a, late1b, gather1a, gather1b, first_v,
+    send2a, send2b, early2a, early2b, middle2a, middle2b, late2a, late2b, gather2a, gather2b,
     next_send, next_recv, kept_v, edge_v, kept_all, edge_all,
     load_sem, pair_ss, pair_rs, ss1, rs1, ss2, rs2, ss3, rs3, ss4, rs4, ss_x, rs_x,
 ):
@@ -67,23 +69,24 @@
     at_z = chip % SIDE
     sibling = {"req": chip * 2 + (1 - core), "grp": group}
 
-    def peer_chip(k):
-        return ((at_y + k // SIDE) % SIDE) * SIDE + (at_z + k % SIDE) % SIDE
-
-    def peer(k):
-        return {"req": peer_chip(k) * 2 + core, "grp": group}
+    def along(axis, k):
+        if axis == 0:
+            chip_at = (at_y + k) % SIDE * SIDE + at_z
+        else:
+            chip_at = at_y * SIDE + (at_z + k) % SIDE
+        return {"req": chip_at * 2 + core, "grp": group}
+
+    places = (at_y, at_z)
 
     def across(k):
         return {"req": member, "grp": (group + k) % GROUPS}
 
     barrier = pltpu.get_barrier_semaphore()
 
-    def greet(k, carry):
-        pl.semaphore_signal(barrier, inc=1, device_id=peer(k), device_id_type=MESH)
-        return carry
-
     pl.semaphore_signal(barrier, inc=1, device_id=sibling, device_id_type=MESH)
-    lax.fori_loop(1, CHIPS, greet, 0)
+    for axis in range(2):
+        for k in range(1, SIDE):
+            pl.semaphore_signal(barrier, inc=1, device_id=along(axis, k), device_id_type=MESH)
     for k in range(1, GROUPS):
         pl.semaphore_signal(barrier, inc=1, device_id=across(k), device_id_type=MESH)
 
@@ -108,7 +111,7 @@
             src_ref=source, dst_ref=target, send_sem=pair_ss.at[slot], recv_sem=pair_rs.at[slot],
             device_id=sibling, device_id_type=MESH)
 
-    pl.semaphore_wait(barrier, CHIPS + GROUPS - 1)
+    pl.semaphore_wait(barrier, 1 + 2 * (SIDE - 1) + GROUPS - 1)
     halves = to_sibling(mixer.at[0:2], pair.at[:, core], 0)
     halves.start()
     shared = [
@@ -193,7 +196,6 @@
     shared[0].wait()
     squares2 = jnp.concatenate([mine[HALF:], theirs[HALF:]], axis=0)
     pick_one = jnp.where(iota((2 * STEPS, EXTRA), 0) % STEPS == 0, 1.0, 0.0).astype(BF16)
-    cut = 512
 
     def folded(low_part, high_part):
         width = low_part.shape[1]
@@ -201,60 +203,134 @@
             [low_part.reshape(CHIPS, ROWS, width), high_part.reshape(CHIPS, ROWS, width)], axis=1
         ).astype(BF16)
 
-    def scatter(source, target, ssem, rsem, c):
-        def copy(k):
-            return pltpu.make_async_remote_copy(
-                src_ref=source.at[c, peer_chip(k)], dst_ref=target.at[c, k], send_sem=ssem.at[c, k],
-                recv_sem=rsem.at[c, k], device_id=peer(k), device_id_type=MESH)
-        return copy
-
-    def gather(target, ssem, rsem, c):
-        def copy(k):
-            return pltpu.make_async_remote_copy(
-                src_ref=target.at[c, chip], dst_ref=target.at[c, chip], send_sem=ssem.at[c, k],
-                recv_sem=rsem.at[c, k], device_id=peer(k), device_id_type=MESH)
-        return copy
-
-    def start_all(copy):
-        def body(k, carry):
-            copy(k).start()
-            return carry
-        lax.fori_loop(1, CHIPS, body, 0)
-
-    def wait_all(copy):
-        def body(k, carry):
-            copy(k).wait_recv()
-            return carry
-        lax.fori_loop(1, CHIPS, body, 0)
-
-    def drain(copy):
-        def body(k, carry):
-            copy(k).wait_send()
-            return carry
-        lax.fori_loop(1, CHIPS, body, 0)
-
-    copy1 = [scatter(send1, recv1, ss1, rs1, c) for c in range(CHUNKS)]
-    copy2 = [gather(gather1, ss2, rs2, c) for c in range(CHUNKS)]
-    copy3 = [scatter(send2, recv2, ss3, rs3, c) for c in range(CHUNKS)]
-    copy4 = [gather(gather2, ss4, rs4, c) for c in range(CHUNKS)]
+    def put(blocks, ref, c, axis):
+        width = blocks.shape[2]
+        blocks = blocks.reshape(SIDE, SIDE, 2 * ROWS, width)
+        if axis == 0:
+            ref[c, :, :, :, 0:width] = blocks
+        else:
+            for y in range(SIDE):
+                ref[c, :, y, :, 0:width] = blocks[y]
+
+    def link(source, target, ssem, rsem, c, axis, stage, k, towards):
+        return pltpu.make_async_remote_copy(
+            src_ref=source, dst_ref=target, send_sem=ssem.at[c, axis, stage, k],
+            recv_sem=rsem.at[c, axis, stage, k], device_id=along(towards, k), device_id_type=MESH)
+
+    class Sum:
+        def __init__(self, sends, early, middle, late, sems):
+            self.sends, self.early, self.middle, self.late, self.sems = sends, early, middle, late, sems
+
+        def first(self, c, axis):
+            return [
+                link(self.sends[axis].at[c, (places[axis] + k) % SIDE], self.early[axis].at[c, k],
+                     *self.sems, c, axis, 0, k, axis)
+                for k in range(1, SIDE)
+            ]
+
+        def second(self, c, axis):
+            other = 1 - axis
+            return [
+                link(self.middle[axis].at[c, (places[other] + k) % SIDE], self.late[axis].at[c, k],
+                     *self.sems, c, axis, 1, k, other)
+                for k in range(1, SIDE)
+            ]
+
+        def begin(self, c, axis):
+            for copy in self.first(c, axis):
+                copy.start()
+
+        def turn(self, c, axis):
+            for copy in self.first(c, axis):
+                copy.wait_recv()
+            sums = self.sends[axis][c, places[axis]].astype(F32)
+            for k in range(1, SIDE):
+                sums = sums + self.early[axis][c, k].astype(F32)
+            self.middle[axis][c] = sums.astype(BF16)
+            for copy in self.second(c, axis):
+                copy.start()
+
+        def end(self, c, axis):
+            for copy in self.second(c, axis):
+                copy.wait_recv()
+            sums = self.middle[axis][c, places[1 - axis]].astype(F32)
+            for k in range(1, SIDE):
+                sums = sums + self.late[axis][c, k].astype(F32)
+            return sums
+
+        def drain(self, c, axis):
+            for copy in self.first(c, axis) + self.second(c, axis):
+                copy.wait_send()
+
+    class Gather:
+        def __init__(self, refs, sems):
+            self.refs, self.sems = refs, sems
+
+        def first(self, c, axis):
+            other = 1 - axis
+            mine_at = self.refs[axis].at[c, places[axis], places[other]]
+            return [link(mine_at, mine_at, *self.sems, c, axis, 0, k, other) for k in range(1, SIDE)]
+
+        def second(self, c, axis):
+            mine_at = self.refs[axis].at[c, places[axis]]
+            return [link(mine_at, mine_at, *self.sems, c, axis, 1, k, axis) for k in range(1, SIDE)]
+
+        def begin(self, c, rows):
+            block = jnp.concatenate([rows[:, 0:FOLD], rows[:, FOLD:]], axis=0).astype(BF16)
+            for axis in range(2):
+                self.refs[axis][c, places[axis], places[1 - axis]] = block[:, axis * LANES:(axis + 1) * LANES]
+                for copy in self.first(c, axis):
+                    copy.start()
+
+        def turn(self, c):
+            for axis in range(2):
+                for copy in self.first(c, axis):
+                    copy.wait_recv()
+                for copy in self.second(c, axis):
+                    copy.start()
+
+        def end(self, c):
+            for axis in range(2):
+                for copy in self.second(c, axis):
+                    copy.wait_recv()
+            pieces = [[], []]
+            for axis in range(2):
+                if axis == 0:
+                    blocks = self.refs[axis][c].astype(F32)
+                else:
+                    blocks = jnp.stack([self.refs[axis][c, :, y] for y in range(SIDE)], axis=0).astype(F32)
+                blocks = blocks.reshape(CHIPS, 2 * ROWS, LANES)
+                pieces[0].append(blocks[:, 0:ROWS].reshape(PART, LANES))
+                pieces[1].append(blocks[:, ROWS:].reshape(PART, LANES))
+            return jnp.concatenate(pieces[0] + pieces[1], axis=1).astype(BF16)
+
+        def drain(self, c):
+            for axis in range(2):
+                for copy in self.first(c, axis) + self.second(c, axis):
+                    copy.wait_send()
+
+    def unfold(left, right):
+        return jnp.concatenate([left[0:ROWS], right[0:ROWS], left[ROWS:], right[ROWS:]], axis=1)
+
+    sum1 = Sum((send1a, send1b), (early1a, early1b), (middle1a, middle1b), (late1a, late1b), (ss1, rs1))
+    spread1 = Gather((gather1a, gather1b), (ss2, rs2))
+    sum2 = Sum((send2a, send2b), (early2a, early2b), (middle2a, middle2b), (late2a, late2b), (ss3, rs3))
+    spread2 = Gather((gather2a, gather2b), (ss4, rs4))
 
     for c in range(CHUNKS):
         part = slice(c * PART, (c + 1) * PART)
         square = dot(squares2[:, part], pick_one, TN)
-        send1[c, :, :, FOLD:] = folded(square, square)
+        square = folded(square, square).reshape(SIDE, SIDE, 2 * ROWS, EXTRA)
+        send1a[c, :, :, :, LANES:] = square
         channels = both[:, part]
-
-        def project(n, carry):
-            at = pl.ds(pl.multiple_of(n * cut, cut), cut)
-            above = pl.ds(pl.multiple_of(FOLD + n * cut, cut), cut)
-            send1[c, :, :, at] = folded(
-                dot(channels, wo[:, :, at].reshape(2 * HALF, cut), TN),
-                dot(channels, wo[:, :, above].reshape(2 * HALF, cut), TN))
-            return carry
-
-        lax.fori_loop(0, FOLD // cut, project, 0)
-        start_all(copy1[c])
-        recv1[c, 0] = send1[c, chip]
+        for axis in range(2):
+            low_at = slice(axis * LANES, (axis + 1) * LANES)
+            high_at = slice(FOLD + axis * LANES, FOLD + (axis + 1) * LANES)
+            put(folded(
+                dot(channels, wo[:, :, low_at].reshape(2 * HALF, LANES), TN),
+                dot(channels, wo[:, :, high_at].reshape(2 * HALF, LANES), TN),
+            ), sum1.sends[axis], c, axis)
+            sum1.begin(c, axis)
 
     acc_column = to_column(accepted[...])
     row32 = iota((REQUESTS, TOKENS), 0)
@@ -300,65 +376,48 @@
     kept_all[group] = kept_v[...]
     edge_all[group] = edge_v[...]
 
-    def total_of(ref, c):
-        def add(k, sums):
-            return sums + ref[c, k].astype(F32)
-        return lax.fori_loop(1, CHIPS, add, ref[c, 0].astype(F32))
-
-    def unfold(block):
-        return jnp.concatenate([block[0:ROWS], block[ROWS:]], axis=1)
-
-    def fold(rows):
-        return jnp.concatenate([rows[:, 0:FOLD], rows[:, FOLD:]], axis=0)
-
     def scaled_norm(rows, gain):
         factor = lax.rsqrt(jnp.mean(rows * rows, axis=1, keepdims=True) + EPSILON)
         return rows * factor * gain
 
-    def all_rows(ref, c):
-        blocks = ref[c].astype(F32)
-        low_part = blocks[:, 0:ROWS].reshape(PART, FOLD)
-        high_part = blocks[:, ROWS:].reshape(PART, FOLD)
-        return jnp.concatenate([low_part, high_part], axis=1).astype(BF16)
-
+    for c in range(CHUNKS):
+        for axis in range(2):
+            sum1.turn(c, axis)
     for load in loads[3:]:
         load.wait()
     for c in range(CHUNKS):
-        wait_all(copy1[c])
-        sums = total_of(recv1, c)
+        left = sum1.end(c, 0)
+        right = sum1.end(c, 1)
         near = res_v[c].astype(F32)
         before = jnp.where(chip % 2 == 0, near[0:ROWS], near[ROWS:])
-        square = sums[0:ROWS, FOLD:FOLD + 1]
-        attn = unfold(sums[:, 0:FOLD]) * lax.rsqrt(square / WIDTH + EPSILON)
+        square = left[0:ROWS, LANES:LANES + 1]
+        attn = unfold(left[:, 0:LANES], right) * lax.rsqrt(square / WIDTH + EPSILON)
         first = (before + attn).astype(BF16).astype(F32)
         first_v[c] = first
-        gather1[c, chip] = fold(scaled_norm(first, gain_mlp[...])).astype(BF16)
-        start_all(copy2[c])
-    for c in range(CHUNKS):
-        drain(copy1[c])
+        spread1.begin(c, scaled_norm(first, gain_mlp[...]))
+    for c in range(CHUNKS):
+        spread1.turn(c)
+    for c in range(CHUNKS):
+        for axis in range(2):
+            sum1.drain(c, axis)
     for copy in shared[1:]:
         copy.wait()
 
     hidden_width = wd.shape[0] * wd.shape[1]
     for c in range(CHUNKS):
-        wait_all(copy2[c])
-        both_parts = dot(wgu[...].reshape(2 * hidden_width, WIDTH), all_rows(gather1, c), NT)
+        both_parts = dot(wgu[...].reshape(2 * hidden_width, WIDTH), spread1.end(c), NT)
         gate = both_parts[0:hidden_width]
         hidden = (gate * jax.nn.sigmoid(gate) * both_parts[hidden_width:]).astype(BF16)
-
-        def lower_part(n, carry):
-            at = pl.ds(pl.multiple_of(n * cut, cut), cut)
-            above = pl.ds(pl.multiple_of(FOLD + n * cut, cut), cut)
-            send2[c, :, :, at] = folded(
-                dot(hidden, wd[:, :, at].reshape(hidden_width, cut), TN),
-                dot(hidden, wd[:, :, above].reshape(hidden_width, cut), TN))
-            return carry
-
-        lax.fori_loop(0, FOLD // cut, lower_part, 0)
-        start_all(copy3[c])
-        recv2[c, 0] = send2[c, chip]
-    for c in range(CHUNKS):
-        drain(copy2[c])
+        for axis in range(2):
+            low_at = slice(axis * LANES, (axis + 1) * LANES)
+            high_at = slice(FOLD + axis * LANES, FOLD + (axis + 1) * LANES)
+            put(folded(
+                dot(hidden, wd[:, :, low_at].reshape(hidden_width, LANES), TN),
+                dot(hidden, wd[:, :, high_at].reshape(hidden_width, LANES), TN),
+            ), sum2.sends[axis], c, axis)
+            sum2.begin(c, axis)
+    for c in range(CHUNKS):
+        spread1.drain(c)
 
     for copy in crossing:
         copy.wait()
@@ -374,17 +433,21 @@
         edge_out[e] = dot(chosen, pool).astype(BF16)
 
     for c in range(CHUNKS):
-        wait_all(copy3[c])
-        second = (first_v[c] + unfold(total_of(recv2, c))).astype(BF16).astype(F32)
-        gather2[c, chip] = fold(scaled_norm(second, gain_next[...])).astype(BF16)
-        start_all(copy4[c])
-    for c in range(CHUNKS):
-        drain(copy3[c])
+        for axis in range(2):
+            sum2.turn(c, axis)
+    for c in range(CHUNKS):
+        down = unfold(sum2.end(c, 0), sum2.end(c, 1))
+        second = (first_v[c] + down).astype(BF16).astype(F32)
+        spread2.begin(c, scaled_norm(second, gain_next[...]))
+    for c in range(CHUNKS):
+        spread2.turn(c)
+    for c in range(CHUNKS):
+        for axis in range(2):
+            sum2.drain(c, axis)
 
     swaps = []
     for c in range(CHUNKS):
-        wait_all(copy4[c])
-        normed = all_rows(gather2, c)
+        normed = spread2.end(c)
         theirs_next = dot(wn[1 - core].reshape(3 * HALF, WIDTH), normed, NT)
         next_send[c] = theirs_next.astype(BF16).reshape(3, HALF, PART)
         swaps.append(to_sibling(next_send.at[c], next_recv.at[c], 7 + c))
@@ -393,10 +456,21 @@
         here = pl.ds(pl.multiple_of(core * MINE + c * PART, PART), PART)
         next_out[:, :, here] = own_next.astype(BF16).reshape(3, HALF, PART)
     for c in range(CHUNKS):
-        drain(copy4[c])
+        spread2.drain(c)
         swaps[c].wait()
         there = pl.ds(pl.multiple_of((1 - core) * MINE + c * PART, PART), PART)
         next_out[:, :, there] = next_recv[c]
+
+
+def sum_buffers(width_a):
+    grids = [(SIDE, SIDE), (SIDE, SIDE), (SIDE,), (SIDE,)]
+    return [
+        pltpu.VMEM((CHUNKS, *grid, 2 * ROWS, width), BF16) for grid in grids for width in (width_a, LANES)
+    ]
+
+
+def gather_buffers():
+    return [pltpu.VMEM((CHUNKS, SIDE, SIDE, 2 * ROWS, LANES), BF16)] * 2
 
 
 def per_device(
@@ -437,13 +511,9 @@
             pltpu.VMEM((HALF + STEPS, TOKENS), BF16),
             pltpu.VMEM((HALF + STEPS, MINE), BF16),
             pltpu.VMEM((HALF + STEPS, MINE), BF16),
-            pltpu.VMEM((CHUNKS, CHIPS, 2 * ROWS, FOLD + EXTRA), BF16),
-            pltpu.VMEM((CHUNKS, CHIPS, 2 * ROWS, FOLD + EXTRA), BF16),
-            pltpu.VMEM((CHUNKS, CHIPS, 2 * ROWS, FOLD), BF16),
+            *sum_buffers(LANES + EXTRA), *gather_buffers(),
             pltpu.VMEM((CHUNKS, ROWS, WIDTH), F32),
-            pltpu.VMEM((CHUNKS, CHIPS, 2 * ROWS, FOLD), BF16),
-            pltpu.VMEM((CHUNKS, CHIPS, 2 * ROWS, FOLD), BF16),
-            pltpu.VMEM((CHUNKS, CHIPS, 2 * ROWS, FOLD), BF16),
+            *sum_buffers(LANES), *gather_buffers(),
             pltpu.VMEM((CHUNKS, 3, HALF, PART), BF16),
             pltpu.VMEM((CHUNKS, 3, HALF, PART), BF16),
             pltpu.VMEM((REQUESTS, HALF, KEYS), BF16),
@@ -451,7 +521,7 @@
             pltpu.VMEM((GROUPS, REQUESTS, HALF, KEYS), BF16),
             pltpu.VMEM((GROUPS, EDGES, REQUESTS, HALF), BF16),
             dma((8 + CHUNKS,)), dma((7 + CHUNKS,)), dma((7 + CHUNKS,)),
-            *[dma((CHUNKS, CHIPS))] * 8,
+            *[dma((CHUNKS, 2, 2, SIDE))] * 8,
             dma((2, GROUPS)), dma((2, GROUPS)),
         ],
         compiler_params=pltpu.CompilerParams(

time: 75.2 us -> 67.7 us (0.900)
  Pallas kernels: 69.1 us -> 61.7 us
    pallas_call x1, Pallas kernels: 69.1 us -> 61.7 us  [per_device(): pl.pallas_call(kernel, name='draft_check', out_shape=(jax.ShapeDtypeStruc...]
where the time goes in v3:
time: 67.7 us; the launch traced here: 67.4 us
  Pallas kernels  61.7 us (91%)
  local copies, waits for them, and re-layouts  2.96 us (4%)
  other arithmetic  2.13 us (3%)
    pallas_call x1, Pallas kernels, per_device(): pl.pallas_call(kernel, name='draft_check', out_shape=(jax.ShapeDtypeStruc...  61.7 us
    unnamed x2, local copies, waits for them, and re-layouts  2.96 us
    convert_element_type x1, other arithmetic, per_device(): kept.astype(F32)  2.13 us

profile of v3, /device:TPU:1, one launch (start us, length us, event | category | flops | bytes accessed | tf_op | source)
XLA Modules:
  0.0 67.4 jit_solution(12152787151295629791)
XLA Ops:
  0.6 61.7 %draft_check.1 = (bf16[3,64,512]{2,1,0:T(8,128)(2,1)}, bf16[32,64,128]{2,1,0:T(8,128)(2,1)}, bf16[3,32,64]{2,1,0:T(8,128)(2,1)}) custom-call(bf16[512,2048]{1,0:T(8,128)(2,1)} %residual.1, bf16[3,64,512]{2,1,0:T(8,128)(2,1)} %bitcast.16, f32[16,128]{1,0:T(8,128)} %bitcast.20, f32[4,64]{1,0:T(4,128)} %taps.1, bf16[3,32,64]{2,1,0:T(8,128)(2,1)} %bitcast.18, ...), custom_call_target="tpu_custom_call" | custom-call | tf_op jit(solution)/shard_map/draft_check/pallas_call | solution.py:484
  62.3 2.1 %convert_element_type.3 = f32[32,64,128]{2,1,0:T(8,128)} convert(bf16[32,64,128]{2,1,0:T(8,128)(2,1)} %get-tuple-element.7) | non-fusion elementwise | flops 262144 | bytes 1572864 | tf_op jit(solution)/shard_map/convert_element_type | solution.py:549
  64.4 1.6 %copy.21 = bf16[512,3,64]{0,2,1:T(8,128)(2,1)} copy(bf16[512,3,64]{0,2,1:T(8,128)(2,1)} %bitcast.17) | data formatting | bytes 393216
  66.0 1.3 %copy.22 = bf16[32,3,64]{2,0,1:T(8,128)(2,1)} copy(bf16[32,3,64]{2,0,1:T(8,128)(2,1)} %bitcast.19) | data formatting | bytes 24576

commit v4 on v3

--- a/solution.py
+++ b/solution.py
@@ -51,15 +51,15 @@
 
 
 def kernel(
-    residual, mixer, floor, taps, edges, state, accepted, home, gain_mixer,
-    w_out, gain_mlp, w_gate, w_up, w_down, gain_next, w_next,
-    next_out, kept_out, edge_out,
-    mix_v, pair, state_v, res_v, wo, wgu, wd, wn,
+    residual, mixer, floor_in, taps_in, edges_in, state, accepted_in, home_in, gain_mixer_in,
+    w_out, gain_mlp_in, w_gate, w_up, w_down, gain_next_in, w_next,
+    next_out, kept_home, edge_out,
+    floor, taps, edges, accepted, home, gain_mixer, gain_mlp, gain_next, kept_out, mix_v, pair, state_v, res_v, wo, wgu, wd, wn,
     query_b, key_b, decay, values, picked, gained_own, gained_send, gained_recv,
     send1a, send1b, early1a, early1b, middle1a, middle1b, late1a, late1b, gather1a, gather1b, first_v,
     send2a, send2b, early2a, early2b, middle2a, middle2b, late2a, late2b, gather2a, gather2b,
     next_send, next_recv, kept_v, edge_v, kept_all, edge_all,
-    load_sem, pair_ss, pair_rs, ss1, rs1, ss2, rs2, ss3, rs3, ss4, rs4, ss_x, rs_x,
+    load_sem, small_sem, pair_ss, pair_rs, ss1, rs1, ss2, rs2, ss_x, rs_x,
 ):
     member = lax.axis_index("req")
     group = lax.axis_index("grp")
@@ -103,7 +103,13 @@
         near = core * MINE + c * PART + chip // 2 * (2 * ROWS)
         loads.append(pltpu.make_async_copy(
             residual.at[pl.ds(pl.multiple_of(near, 2 * ROWS), 2 * ROWS)], res_v.at[c], load_sem.at[8 + c]))
-    for load in loads:
+    smalls = [
+        pltpu.make_async_copy(source, target, small_sem.at[i])
+        for i, (source, target) in enumerate((
+            (taps_in, taps), (edges_in, edges), (floor_in, floor), (gain_mixer_in, gain_mixer),
+            (accepted_in, accepted), (home_in, home), (gain_mlp_in, gain_mlp), (gain_next_in, gain_next)))
+    ]
+    for load in loads[:1] + smalls + loads[1:]:
         load.start()
 
     def to_sibling(source, target, slot):
@@ -124,7 +130,8 @@
     for copy in shared:
         copy.start()
 
-    loads[0].wait()
+    for load in smalls + loads[:1]:
+        load.wait()
     lane = iota((1, TOKENS), 1)
     step_of = lane % STEPS
     inputs_raw = mix_v[2]
@@ -214,8 +221,8 @@
 
     def link(source, target, ssem, rsem, c, axis, stage, k, towards):
         return pltpu.make_async_remote_copy(
-            src_ref=source, dst_ref=target, send_sem=ssem.at[c, axis, stage, k],
-            recv_sem=rsem.at[c, axis, stage, k], device_id=along(towards, k), device_id_type=MESH)
+            src_ref=source, dst_ref=target, send_sem=ssem.at[c, axis, stage, k - 1],
+            recv_sem=rsem.at[c, axis, stage, k - 1], device_id=along(towards, k), device_id_type=MESH)
 
     class Sum:
         def __init__(self, sends, early, middle, late, sems):
@@ -314,8 +321,8 @@
 
     sum1 = Sum((send1a, send1b), (early1a, early1b), (middle1a, middle1b), (late1a, late1b), (ss1, rs1))
     spread1 = Gather((gather1a, gather1b), (ss2, rs2))
-    sum2 = Sum((send2a, send2b), (early2a, early2b), (middle2a, middle2b), (late2a, late2b), (ss3, rs3))
-    spread2 = Gather((gather2a, gather2b), (ss4, rs4))
+    sum2 = Sum((send2a, send2b), (early2a, early2b), (middle2a, middle2b), (late2a, late2b), (ss1, rs1))
+    spread2 = Gather((gather2a, gather2b), (ss2, rs2))
 
     for c in range(CHUNKS):
         part = slice(c * PART, (c + 1) * PART)
@@ -365,8 +372,8 @@
     def cross(k):
         return [
             pltpu.make_async_remote_copy(
-                src_ref=source, dst_ref=target.at[group], send_sem=ss_x.at[slot, k],
-                recv_sem=rs_x.at[slot, k], device_id=across(k), device_id_type=MESH)
+                src_ref=source, dst_ref=target.at[group], send_sem=ss_x.at[slot, k - 1],
+                recv_sem=rs_x.at[slot, k - 1], device_id=across(k), device_id_type=MESH)
             for slot, (source, target) in enumerate(((kept_v, kept_all), (edge_v, edge_all)))
         ]
 
@@ -419,28 +426,31 @@
     for c in range(CHUNKS):
         spread1.drain(c)
 
+    for c in range(CHUNKS):
+        for axis in range(2):
+            sum2.turn(c, axis)
+    for c in range(CHUNKS):
+        down = unfold(sum2.end(c, 0), sum2.end(c, 1))
+        second = (first_v[c] + down).astype(BF16).astype(F32)
+        spread2.begin(c, scaled_norm(second, gain_next[...]))
+    for c in range(CHUNKS):
+        spread2.turn(c)
+
     for copy in crossing:
         copy.wait()
     home_row = home[...]
     source_lane = iota((1, GROUPS * REQUESTS), 1)
     for i in range(REQUESTS):
         found = jnp.max(jnp.where(home_row == group * REQUESTS + i, source_lane, 0))
-        kept_out[i] = kept_all[found // REQUESTS, found % REQUESTS]
+        kept_out[i] = kept_all[found // REQUESTS, found % REQUESTS].astype(F32)
+    leaving = pltpu.make_async_copy(kept_out, kept_home, load_sem.at[8 + CHUNKS])
+    leaving.start()
     target_row = iota((REQUESTS, GROUPS * REQUESTS), 0) + group * REQUESTS
     chosen = jnp.where(home_row == target_row, 1.0, 0.0).astype(BF16)
     for e in range(EDGES):
         pool = edge_all[:, e].reshape(GROUPS * REQUESTS, HALF)
         edge_out[e] = dot(chosen, pool).astype(BF16)
 
-    for c in range(CHUNKS):
-        for axis in range(2):
-            sum2.turn(c, axis)
-    for c in range(CHUNKS):
-        down = unfold(sum2.end(c, 0), sum2.end(c, 1))
-        second = (first_v[c] + down).astype(BF16).astype(F32)
-        spread2.begin(c, scaled_norm(second, gain_next[...]))
-    for c in range(CHUNKS):
-        spread2.turn(c)
     for c in range(CHUNKS):
         for axis in range(2):
             sum2.drain(c, axis)
@@ -460,6 +470,16 @@
         swaps[c].wait()
         there = pl.ds(pl.multiple_of((1 - core) * MINE + c * PART, PART), PART)
         next_out[:, :, there] = next_recv[c]
+    leaving.wait()
+
+
+def finish(next_in, kept_in, edge_in, next_out, kept_out, edge_out, sems):
+    pairs = ((kept_in, kept_out), (next_in, next_out), (edge_in, edge_out))
+    copies = [pltpu.make_async_copy(source, target, sems.at[i]) for i, (source, target) in enumerate(pairs)]
+    for copy in copies:
+        copy.start()
+    for copy in copies:
+        copy.wait()
 
 
 def sum_buffers(width_a):
@@ -481,20 +501,27 @@
     anywhere = pl.BlockSpec(memory_space=pl.ANY)
     vmem = pl.BlockSpec(memory_space=pltpu.VMEM)
     dma = pltpu.SemaphoreType.DMA
-    next_flat, kept, kept_edges = pl.pallas_call(
+    outputs = (
+        jax.ShapeDtypeStruct((3, HALF, TOKENS), BF16),
+        jax.ShapeDtypeStruct((REQUESTS, HALF, KEYS), F32),
+        jax.ShapeDtypeStruct((EDGES, REQUESTS, HALF), BF16),
+    )
+    results = pl.pallas_call(
         kernel,
         name="draft_check",
-        out_shape=(
-            jax.ShapeDtypeStruct((3, HALF, TOKENS), BF16),
-            jax.ShapeDtypeStruct((REQUESTS, HALF, KEYS), BF16),
-            jax.ShapeDtypeStruct((EDGES, REQUESTS, HALF), BF16),
-        ),
-        in_specs=[
-            anywhere, anywhere, vmem, vmem, vmem, anywhere, vmem, vmem, vmem,
-            anywhere, vmem, anywhere, anywhere, anywhere, vmem, anywhere,
-        ],
-        out_specs=(vmem, vmem, vmem),
+        out_shape=outputs,
+        in_specs=[anywhere] * 16,
+        out_specs=(vmem, anywhere, vmem),
         scratch_shapes=[
+            pltpu.VMEM((CHIPS, KEYS), F32),
+            pltpu.VMEM((TAPS, HALF), F32),
+            pltpu.VMEM((EDGES, REQUESTS, HALF), BF16),
+            pltpu.VMEM((1, REQUESTS), jnp.int32),
+            pltpu.VMEM((1, GROUPS * REQUESTS), jnp.int32),
+            pltpu.VMEM((1, HALF), F32),
+            pltpu.VMEM((1, WIDTH), F32),
+            pltpu.VMEM((1, WIDTH), F32),
+            pltpu.VMEM((REQUESTS, HALF, KEYS), F32),
             pltpu.VMEM((3, HALF, TOKENS), BF16),
             pltpu.VMEM((2, 2, HALF, TOKENS), BF16),
             pltpu.VMEM((REQUESTS, HALF, KEYS), F32),
@@ -520,9 +547,9 @@
             pltpu.VMEM((EDGES, REQUESTS, HALF), BF16),
             pltpu.VMEM((GROUPS, REQUESTS, HALF, KEYS), BF16),
             pltpu.VMEM((GROUPS, EDGES, REQUESTS, HALF), BF16),
-            dma((8 + CHUNKS,)), dma((7 + CHUNKS,)), dma((7 + CHUNKS,)),
-            *[dma((CHUNKS, 2, 2, SIDE))] * 8,
-            dma((2, GROUPS)), dma((2, GROUPS)),
+            dma((9 + CHUNKS,)), dma((8,)), dma((7 + CHUNKS,)), dma((7 + CHUNKS,)),
+            *[dma((CHUNKS, 2, 2, SIDE - 1))] * 4,
+            dma((2, GROUPS - 1)), dma((2, GROUPS - 1)),
         ],
         compiler_params=pltpu.CompilerParams(
             collective_id=0, has_side_effects=True, vmem_limit_bytes=56 * 2**20),
@@ -544,11 +571,16 @@
         gain_next.reshape(1, -1),
         w_next.transpose(1, 2, 0),
     )
-    return (
-        next_flat.transpose(2, 0, 1),
-        kept.astype(F32),
-        kept_edges.transpose(1, 0, 2),
-    )
+    next_flat, kept, kept_edges = pl.pallas_call(
+        finish,
+        name="finish",
+        out_shape=outputs,
+        in_specs=[anywhere] * 3,
+        out_specs=(anywhere,) * 3,
+        scratch_shapes=[dma((3,))],
+        compiler_params=pltpu.CompilerParams(vmem_limit_bytes=56 * 2**20),
+    )(*results)
+    return next_flat.transpose(2, 0, 1), kept, kept_edges.transpose(1, 0, 2)
 
 
 def solution(mesh):

time: 67.7 us -> 99.7 us (1.47)
  Pallas kernels: 61.7 us -> 98.9 us
  local copies, waits for them, and re-layouts: 2.96 us -> 0 us
  other arithmetic: 2.13 us -> 0 us
    pallas_call x1 -> x2, Pallas kernels: 61.7 us -> 98.9 us  [the longest x1 59.3 us: per_device(): pl.pallas_call(kernel, name='draft_check', out_shape=outputs, in_specs=[a...]
    unnamed x2 -> x0, local copies, waits for them, and re-layouts: 2.96 us -> none
    convert_element_type x1 -> x0, other arithmetic: 2.13 us -> none  [per_device(): kept.astype(F32)]
where the time goes in v4:
time: 99.7 us; the launch traced here: 99.6 us
  Pallas kernels  98.9 us (99%)
    pallas_call x1, Pallas kernels, per_device(): pl.pallas_call(kernel, name='draft_check', out_shape=outputs, in_specs=[a...  59.3 us
    pallas_call x1, Pallas kernels, per_device(): pl.pallas_call(finish, name='finish', out_shape=outputs, in_specs=[anywhe...  39.6 us

profile of v4, /device:TPU:1, one launch (start us, length us, event | category | flops | bytes accessed | tf_op | source)
XLA Modules:
  0.0 99.6 jit_solution(6202149202719093033)
XLA Ops:
  0.6 59.3 %draft_check.1 = (bf16[3,64,512]{2,1,0:T(8,128)(2,1)}, f32[32,64,128]{2,1,0:T(8,128)}, bf16[3,32,64]{2,1,0:T(8,128)(2,1)}) custom-call(bf16[512,2048]{1,0:T(8,128)(2,1)} %residual.1, bf16[3,64,512]{2,1,0:T(8,128)(2,1)} %bitcast.16, f32[16,128]{1,0:T(8,128)} %bitcast.18, f32[4,64]{1,0:T(4,128)} %taps_in.1, bf16[3,32,64]{2,1,0:T(8,128)(2,1)} %bitcast.17, ...), custom_call_target="tpu_custom_call" | custom-call | tf_op jit(solution)/shard_map/draft_check/pallas_call | solution.py:509
  60.0 39.6 %finish.1 = (bf16[3,64,512]{2,1,0:T(8,128)(2,1)}, f32[32,64,128]{2,1,0:T(8,128)}, bf16[3,32,64]{2,1,0:T(8,128)(2,1)}) custom-call(bf16[3,64,512]{2,1,0:T(8,128)(2,1)} %get-tuple-element.9.next_in, f32[32,64,128]{2,1,0:T(8,128)} %get-tuple-element.10.kept_in, bf16[3,32,64]{2,1,0:T(8,128)(2,1)} %get-tuple-element.11.edge_in), custom_call_target="tpu_custom_call" | custom-call | tf_op jit(solution)/shard_map/finish/pallas_call | solution.py:574

commit v5 on v4

--- a/solution.py
+++ b/solution.py
@@ -473,12 +473,22 @@
     leaving.wait()
 
 
-def finish(next_in, kept_in, edge_in, next_out, kept_out, edge_out, sems):
-    pairs = ((kept_in, kept_out), (next_in, next_out), (edge_in, edge_out))
-    copies = [pltpu.make_async_copy(source, target, sems.at[i]) for i, (source, target) in enumerate(pairs)]
-    for copy in copies:
+PIECES = 4
+PIECE = REQUESTS // PIECES
+
+
+def finish(next_in, kept_in, edge_in, next_out, kept_out, edge_out, next_v, kept_v, edge_v, in_sems, out_sems):
+    parts = [slice(i * PIECE, (i + 1) * PIECE) for i in range(PIECES)]
+    routes = [(kept_in.at[part], kept_v.at[part], kept_out.at[part]) for part in parts]
+    routes += [(next_in, next_v, next_out), (edge_in, edge_v, edge_out)]
+    arrive = [pltpu.make_async_copy(a, b, in_sems.at[i]) for i, (a, b, _) in enumerate(routes)]
+    leave = [pltpu.make_async_copy(b, c, out_sems.at[i]) for i, (_, b, c) in enumerate(routes)]
+    for copy in arrive:
         copy.start()
-    for copy in copies:
+    for copy, further in zip(arrive, leave):
+        copy.wait()
+        further.start()
+    for copy in leave:
         copy.wait()
 
 
@@ -577,7 +587,10 @@
         out_shape=outputs,
         in_specs=[anywhere] * 3,
         out_specs=(anywhere,) * 3,
-        scratch_shapes=[dma((3,))],
+        scratch_shapes=[
+            *[pltpu.VMEM(output.shape, output.dtype) for output in outputs],
+            dma((PIECES + 2,)), dma((PIECES + 2,)),
+        ],
         compiler_params=pltpu.CompilerParams(vmem_limit_bytes=56 * 2**20),
     )(*results)
     return next_flat.transpose(2, 0, 1), kept, kept_edges.transpose(1, 0, 2)

time: 99.7 us -> 62.2 us (0.62)
  Pallas kernels: 98.9 us -> 61.4 us
    pallas_call x1, Pallas kernels: 39.6 us -> 2.08 us  [per_device(): pl.pallas_call(finish, name='finish', out_shape=outputs, in_specs=[anywhe...]
where the time goes in v5:
time: 62.2 us; the launch traced here: 62.1 us
  Pallas kernels  61.4 us (99%)
  between operations  0.65 us (1%)
    pallas_call x1, Pallas kernels, per_device(): pl.pallas_call(kernel, name='draft_check', out_shape=outputs, in_specs=[a...  59.3 us
    pallas_call x1, Pallas kernels, per_device(): pl.pallas_call(finish, name='finish', out_shape=outputs, in_specs=[anywhe...  2.08 us

profile of v5, /device:TPU:1, one launch (start us, length us, event | category | flops | bytes accessed | tf_op | source)
XLA Modules:
  0.0 62.1 jit_solution(2126567574733531732)
XLA Ops:
  0.6 59.3 %draft_check.1 = (bf16[3,64,512]{2,1,0:T(8,128)(2,1)}, f32[32,64,128]{2,1,0:T(8,128)}, bf16[3,32,64]{2,1,0:T(8,128)(2,1)}) custom-call(bf16[512,2048]{1,0:T(8,128)(2,1)} %residual.1, bf16[3,64,512]{2,1,0:T(8,128)(2,1)} %bitcast.16, f32[16,128]{1,0:T(8,128)} %bitcast.18, f32[4,64]{1,0:T(4,128)} %taps_in.1, bf16[3,32,64]{2,1,0:T(8,128)(2,1)} %bitcast.17, ...), custom_call_target="tpu_custom_call" | custom-call | tf_op jit(solution)/shard_map/draft_check/pallas_call | solution.py:519
  60.0 2.1 %finish.1 = (bf16[3,64,512]{2,1,0:T(8,128)(2,1)}, f32[32,64,128]{2,1,0:T(8,128)}, bf16[3,32,64]{2,1,0:T(8,128)(2,1)}) custom-call(bf16[3,64,512]{2,1,0:T(8,128)(2,1)} %get-tuple-element.9.next_in, f32[32,64,128]{2,1,0:T(8,128)} %get-tuple-element.10.kept_in, bf16[3,32,64]{2,1,0:T(8,128)(2,1)} %get-tuple-element.11.edge_in), custom_call_target="tpu_custom_call" | custom-call | tf_op jit(solution)/shard_map/finish/pallas_call | solution.py:584

commit v6 on v5

--- a/solution.py
+++ b/solution.py
@@ -76,8 +76,6 @@
             chip_at = at_y * SIDE + (at_z + k) % SIDE
         return {"req": chip_at * 2 + core, "grp": group}
 
-    places = (at_y, at_z)
-
     def across(k):
         return {"req": member, "grp": (group + k) % GROUPS}
 
@@ -210,36 +208,47 @@
             [low_part.reshape(CHIPS, ROWS, width), high_part.reshape(CHIPS, ROWS, width)], axis=1
         ).astype(BF16)
 
-    def put(blocks, ref, c, axis):
+    def spot(y, z, axis, absolute):
+        if absolute:
+            y, z = (y - at_y + SIDE) % SIDE, (z - at_z + SIDE) % SIDE
+        return (y, z) if axis == 0 else (z, y)
+
+    def put(blocks, ref, c, axis, absolute):
         width = blocks.shape[2]
-        blocks = blocks.reshape(SIDE, SIDE, 2 * ROWS, width)
-        if axis == 0:
-            ref[c, :, :, :, 0:width] = blocks
-        else:
-            for y in range(SIDE):
-                ref[c, :, y, :, 0:width] = blocks[y]
+        for y in range(SIDE):
+            for z in range(SIDE):
+                i, j = spot(y, z, axis, absolute)
+                ref[c, i, j, :, 0:width] = blocks[y * SIDE + z]
 
     def link(source, target, ssem, rsem, c, axis, stage, k, towards):
         return pltpu.make_async_remote_copy(
             src_ref=source, dst_ref=target, send_sem=ssem.at[c, axis, stage, k - 1],
             recv_sem=rsem.at[c, axis, stage, k - 1], device_id=along(towards, k), device_id_type=MESH)
 
+    far = slice(1, SIDE)
+
     class Sum:
         def __init__(self, sends, early, middle, late, sems):
             self.sends, self.early, self.middle, self.late, self.sems = sends, early, middle, late, sems
 
         def first(self, c, axis):
             return [
-                link(self.sends[axis].at[c, (places[axis] + k) % SIDE], self.early[axis].at[c, k],
+                link(self.sends[axis].at[c, k, far], self.early[axis].at[c, k, far],
                      *self.sems, c, axis, 0, k, axis)
                 for k in range(1, SIDE)
             ]
 
+        def near(self, c, axis):
+            return [
+                link(self.sends[axis].at[c, k, 0], self.early[axis].at[c, k, 0],
+                     *self.sems, c, axis, 2, k, axis)
+                for k in range(1, SIDE)
+            ]
+
         def second(self, c, axis):
-            other = 1 - axis
             return [
-                link(self.middle[axis].at[c, (places[other] + k) % SIDE], self.late[axis].at[c, k],
-                     *self.sems, c, axis, 1, k, other)
+                link(self.middle[axis].at[c, k], self.late[axis].at[c, k],
+                     *self.sems, c, axis, 1, k, 1 - axis)
                 for k in range(1, SIDE)
             ]
 
@@ -250,23 +259,24 @@
         def turn(self, c, axis):
             for copy in self.first(c, axis):
                 copy.wait_recv()
-            sums = self.sends[axis][c, places[axis]].astype(F32)
+            sums = self.sends[axis][c, 0, far].astype(F32)
             for k in range(1, SIDE):
-                sums = sums + self.early[axis][c, k].astype(F32)
-            self.middle[axis][c] = sums.astype(BF16)
-            for copy in self.second(c, axis):
+                sums = sums + self.early[axis][c, k, far].astype(F32)
+            self.middle[axis][c, far] = sums.astype(BF16)
+            for copy in self.second(c, axis) + self.near(c, axis):
                 copy.start()
 
         def end(self, c, axis):
-            for copy in self.second(c, axis):
+            for copy in self.second(c, axis) + self.near(c, axis):
                 copy.wait_recv()
-            sums = self.middle[axis][c, places[1 - axis]].astype(F32)
+            sums = self.sends[axis][c, 0, 0].astype(F32)
             for k in range(1, SIDE):
+                sums = sums + self.early[axis][c, k, 0].astype(F32)
                 sums = sums + self.late[axis][c, k].astype(F32)
             return sums
 
         def drain(self, c, axis):
-            for copy in self.first(c, axis) + self.second(c, axis):
+            for copy in self.first(c, axis) + self.second(c, axis) + self.near(c, axis):
                 copy.wait_send()
 
     class Gather:
@@ -274,19 +284,34 @@
             self.refs, self.sems = refs, sems
 
         def first(self, c, axis):
-            other = 1 - axis
-            mine_at = self.refs[axis].at[c, places[axis], places[other]]
-            return [link(mine_at, mine_at, *self.sems, c, axis, 0, k, other) for k in range(1, SIDE)]
+            ref = self.refs[axis]
+            return [
+                link(ref.at[c, 0, 0], ref.at[c, 0, SIDE - k], *self.sems, c, axis, 0, k, 1 - axis)
+                for k in range(1, SIDE)
+            ]
+
+        def near(self, c, axis):
+            ref = self.refs[axis]
+            return [
+                link(ref.at[c, 0, 0], ref.at[c, SIDE - k, 0], *self.sems, c, axis, 2, k, axis)
+                for k in range(1, SIDE)
+            ]
 
         def second(self, c, axis):
-            mine_at = self.refs[axis].at[c, places[axis]]
-            return [link(mine_at, mine_at, *self.sems, c, axis, 1, k, axis) for k in range(1, SIDE)]
+            ref = self.refs[axis]
+            return [
+                link(ref.at[c, 0, far], ref.at[c, SIDE - k, far], *self.sems, c, axis, 1, k, axis)
+                for k in range(1, SIDE)
+            ]
 
         def begin(self, c, rows):
             block = jnp.concatenate([rows[:, 0:FOLD], rows[:, FOLD:]], axis=0).astype(BF16)
             for axis in range(2):
-                self.refs[axis][c, places[axis], places[1 - axis]] = block[:, axis * LANES:(axis + 1) * LANES]
+                self.refs[axis][c, 0, 0] = block[:, axis * LANES:(axis + 1) * LANES]
                 for copy in self.first(c, axis):
+                    copy.start()
+            for axis in range(2):
+                for copy in self.near(c, axis):
                     copy.start()
 
         def turn(self, c):
@@ -296,24 +321,24 @@
                 for copy in self.second(c, axis):
                     copy.start()
 
-        def end(self, c):
+        def end(self, c, absolute):
             for axis in range(2):
-                for copy in self.second(c, axis):
+                for copy in self.near(c, axis) + self.second(c, axis):
                     copy.wait_recv()
-            pieces = [[], []]
+            rows = [[], []]
             for axis in range(2):
-                if axis == 0:
-                    blocks = self.refs[axis][c].astype(F32)
-                else:
-                    blocks = jnp.stack([self.refs[axis][c, :, y] for y in range(SIDE)], axis=0).astype(F32)
-                blocks = blocks.reshape(CHIPS, 2 * ROWS, LANES)
-                pieces[0].append(blocks[:, 0:ROWS].reshape(PART, LANES))
-                pieces[1].append(blocks[:, ROWS:].reshape(PART, LANES))
-            return jnp.concatenate(pieces[0] + pieces[1], axis=1).astype(BF16)
+                blocks = []
+                for y in range(SIDE):
+                    for z in range(SIDE):
+                        i, j = spot(y, z, axis, absolute)
+                        blocks.append(self.refs[axis][c, i, j].astype(F32))
+                rows[0].append(jnp.concatenate([block[0:ROWS] for block in blocks], axis=0))
+                rows[1].append(jnp.concatenate([block[ROWS:] for block in blocks], axis=0))
+            return jnp.concatenate(rows[0] + rows[1], axis=1).astype(BF16)
 
         def drain(self, c):
             for axis in range(2):
-                for copy in self.first(c, axis) + self.second(c, axis):
+                for copy in self.first(c, axis) + self.near(c, axis) + self.second(c, axis):
                     copy.wait_send()
 
     def unfold(left, right):
@@ -327,16 +352,17 @@
     for c in range(CHUNKS):
         part = slice(c * PART, (c + 1) * PART)
         square = dot(squares2[:, part], pick_one, TN)
-        square = folded(square, square).reshape(SIDE, SIDE, 2 * ROWS, EXTRA)
-        send1a[c, :, :, :, LANES:] = square
+        square = folded(square, square)
         channels = both[:, part]
         for axis in range(2):
             low_at = slice(axis * LANES, (axis + 1) * LANES)
             high_at = slice(FOLD + axis * LANES, FOLD + (axis + 1) * LANES)
-            put(folded(
+            terms = folded(
                 dot(channels, wo[:, :, low_at].reshape(2 * HALF, LANES), TN),
-                dot(channels, wo[:, :, high_at].reshape(2 * HALF, LANES), TN),
-            ), sum1.sends[axis], c, axis)
+                dot(channels, wo[:, :, high_at].reshape(2 * HALF, LANES), TN))
+            if axis == 0:
+                terms = jnp.concatenate([terms, square], axis=2)
+            put(terms, sum1.sends[axis], c, axis, True)
             sum1.begin(c, axis)
 
     acc_column = to_column(accepted[...])
@@ -412,7 +438,7 @@
 
     hidden_width = wd.shape[0] * wd.shape[1]
     for c in range(CHUNKS):
-        both_parts = dot(wgu[...].reshape(2 * hidden_width, WIDTH), spread1.end(c), NT)
+        both_parts = dot(wgu[...].reshape(2 * hidden_width, WIDTH), spread1.end(c, False), NT)
         gate = both_parts[0:hidden_width]
         hidden = (gate * jax.nn.sigmoid(gate) * both_parts[hidden_width:]).astype(BF16)
         for axis in range(2):
@@ -421,7 +447,7 @@
             put(folded(
                 dot(hidden, wd[:, :, low_at].reshape(hidden_width, LANES), TN),
                 dot(hidden, wd[:, :, high_at].reshape(hidden_width, LANES), TN),
-            ), sum2.sends[axis], c, axis)
+            ), sum2.sends[axis], c, axis, False)
             sum2.begin(c, axis)
     for c in range(CHUNKS):
         spread1.drain(c)
@@ -457,7 +483,7 @@
 
     swaps = []
     for c in range(CHUNKS):
-        normed = spread2.end(c)
+        normed = spread2.end(c, True)
         theirs_next = dot(wn[1 - core].reshape(3 * HALF, WIDTH), normed, NT)
         next_send[c] = theirs_next.astype(BF16).reshape(3, HALF, PART)
         swaps.append(to_sibling(next_send.at[c], next_recv.at[c], 7 + c))
@@ -558,7 +584,7 @@
             pltpu.VMEM((GROUPS, REQUESTS, HALF, KEYS), BF16),
             pltpu.VMEM((GROUPS, EDGES, REQUESTS, HALF), BF16),
             dma((9 + CHUNKS,)), dma((8,)), dma((7 + CHUNKS,)), dma((7 + CHUNKS,)),
-            *[dma((CHUNKS, 2, 2, SIDE - 1))] * 4,
+            *[dma((CHUNKS, 2, 3, SIDE - 1))] * 4,
             dma((2, GROUPS - 1)), dma((2, GROUPS - 1)),
         ],
         compiler_params=pltpu.CompilerParams(

time: 62.2 us -> 61.8 us (level)
  no operation moved by 1% of the time
where the time goes in v6:
time: 61.8 us; the launch traced here: 61.7 us
  Pallas kernels  61 us (99%)
  between operations  0.65 us (1%)
    pallas_call x1, Pallas kernels, per_device(): pl.pallas_call(kernel, name='draft_check', out_shape=outputs, in_specs=[a...  58.9 us
    pallas_call x1, Pallas kernels, per_device(): pl.pallas_call(finish, name='finish', out_shape=outputs, in_specs=[anywhe...  2.08 us

profile of v6, /device:TPU:1, one launch (start us, length us, event | category | flops | bytes accessed | tf_op | source)
XLA Modules:
  0.0 61.7 jit_solution(627648062306392299)
XLA Ops:
  0.6 58.9 %draft_check.1 = (bf16[3,64,512]{2,1,0:T(8,128)(2,1)}, f32[32,64,128]{2,1,0:T(8,128)}, bf16[3,32,64]{2,1,0:T(8,128)(2,1)}) custom-call(bf16[512,2048]{1,0:T(8,128)(2,1)} %residual.1, bf16[3,64,512]{2,1,0:T(8,128)(2,1)} %bitcast.16, f32[16,128]{1,0:T(8,128)} %bitcast.18, f32[4,64]{1,0:T(4,128)} %taps_in.1, bf16[3,32,64]{2,1,0:T(8,128)(2,1)} %bitcast.17, ...), custom_call_target="tpu_custom_call" | custom-call | tf_op jit(solution)/shard_map/draft_check/pallas_call | solution.py:545
  59.6 2.1 %finish.1 = (bf16[3,64,512]{2,1,0:T(8,128)(2,1)}, f32[32,64,128]{2,1,0:T(8,128)}, bf16[3,32,64]{2,1,0:T(8,128)(2,1)}) custom-call(bf16[3,64,512]{2,1,0:T(8,128)(2,1)} %get-tuple-element.9.next_in, f32[32,64,128]{2,1,0:T(8,128)} %get-tuple-element.10.kept_in, bf16[3,32,64]{2,1,0:T(8,128)(2,1)} %get-tuple-element.11.edge_in), custom_call_target="tpu_custom_call" | custom-call | tf_op jit(solution)/shard_map/finish/pallas_call | solution.py:610

commit v7 on v6

--- a/solution.py
+++ b/solution.py
@@ -150,8 +150,11 @@
     pair[:, core] = mix_v[0:2]
     floor_row = floor[pl.ds(chip, 1), :]
     low = to_column(floor_row)
+    gain_column = to_column(gain_mixer[...])
     halves.wait()
-    for tile in range(TOKENS // TILE):
+    loads[1].wait()
+
+    def gates(tile):
         at = slice(tile * TILE, (tile + 1) * TILE)
         step_t = iota((KEYS, TILE), 1) % STEPS
         q_pre = pair[0, :, :, at].reshape(KEYS, TILE).astype(F32)
@@ -166,10 +169,7 @@
         query_b[:, at] = (query * run).astype(BF16)
         key_b[:, at] = (keyed / run).astype(BF16)
 
-    loads[1].wait()
-    gain_column = to_column(gain_mixer[...])
-    squares = []
-    for tile in range(TOKENS // TILE):
+    def recurrence(tile):
         at = slice(tile * TILE, (tile + 1) * TILE)
         q_t = query_b[:, at]
         begin = state_v[tile * TILE_REQ:(tile + 1) * TILE_REQ].astype(BF16).reshape(TILE_REQ * HALF, KEYS)
@@ -186,20 +186,15 @@
         square = jnp.sum(total * total, axis=0, keepdims=True)
         gained_own[HALF:HALF + STEPS, at] = jnp.broadcast_to(square, (STEPS, TILE)).astype(BF16)
 
-    own_lanes = pl.ds(pl.multiple_of(core * MINE, MINE), MINE)
-    other_lanes = pl.ds(pl.multiple_of((1 - core) * MINE, MINE), MINE)
-    gained_send[...] = gained_own[:, other_lanes]
-    swap = to_sibling(gained_send, gained_recv, 6)
-    swap.start()
-    mine = gained_own[:, own_lanes]
-    swap.wait()
-    theirs = gained_recv[...]
-    lower = jnp.where(core == 0, mine[0:HALF], theirs[0:HALF])
-    upper = jnp.where(core == 0, theirs[0:HALF], mine[0:HALF])
-    both = jnp.concatenate([lower, upper], axis=0)
-    loads[2].wait()
-    shared[0].wait()
-    squares2 = jnp.concatenate([mine[HALF:], theirs[HALF:]], axis=0)
+    gained_swaps = []
+    for c in range(CHUNKS):
+        for tile in (c, CHUNKS + c):
+            gates(tile)
+            recurrence(tile)
+        other_lanes = pl.ds(pl.multiple_of((1 - core) * MINE + c * PART, PART), PART)
+        gained_send[c] = gained_own[:, other_lanes]
+        gained_swaps.append(to_sibling(gained_send.at[c], gained_recv.at[c], 6 + c))
+        gained_swaps[c].start()
     pick_one = jnp.where(iota((2 * STEPS, EXTRA), 0) % STEPS == 0, 1.0, 0.0).astype(BF16)
 
     def folded(low_part, high_part):
@@ -222,10 +217,14 @@
 
     def link(source, target, ssem, rsem, c, axis, stage, k, towards):
         return pltpu.make_async_remote_copy(
-            src_ref=source, dst_ref=target, send_sem=ssem.at[c, axis, stage, k - 1],
-            recv_sem=rsem.at[c, axis, stage, k - 1], device_id=along(towards, k), device_id_type=MESH)
+            src_ref=source, dst_ref=target, send_sem=ssem.at[c, axis, stage],
+            recv_sem=rsem.at[c, axis, stage], device_id=along(towards, k), device_id_type=MESH)
 
     far = slice(1, SIDE)
+
+    def wait_for(region, sem):
+        pltpu.make_async_copy(region, region, sem).wait()
+
 
     class Sum:
         def __init__(self, sends, early, middle, late, sems):
@@ -257,8 +256,7 @@
                 copy.start()
 
         def turn(self, c, axis):
-            for copy in self.first(c, axis):
-                copy.wait_recv()
+            wait_for(self.early[axis].at[c, far, far], self.sems[1].at[c, axis, 0])
             sums = self.sends[axis][c, 0, far].astype(F32)
             for k in range(1, SIDE):
                 sums = sums + self.early[axis][c, k, far].astype(F32)
@@ -267,8 +265,8 @@
                 copy.start()
 
         def end(self, c, axis):
-            for copy in self.second(c, axis) + self.near(c, axis):
-                copy.wait_recv()
+            wait_for(self.late[axis].at[c, far], self.sems[1].at[c, axis, 1])
+            wait_for(self.early[axis].at[c, far, 0], self.sems[1].at[c, axis, 2])
             sums = self.sends[axis][c, 0, 0].astype(F32)
             for k in range(1, SIDE):
                 sums = sums + self.early[axis][c, k, 0].astype(F32)
@@ -276,8 +274,9 @@
             return sums
 
         def drain(self, c, axis):
-            for copy in self.first(c, axis) + self.second(c, axis) + self.near(c, axis):
-                copy.wait_send()
+            wait_for(self.sends[axis].at[c, far, far], self.sems[0].at[c, axis, 0])
+            wait_for(self.middle[axis].at[c, far], self.sems[0].at[c, axis, 1])
+            wait_for(self.sends[axis].at[c, far, 0], self.sems[0].at[c, axis, 2])
 
     class Gather:
         def __init__(self, refs, sems):
@@ -316,15 +315,14 @@
 
         def turn(self, c):
             for axis in range(2):
-                for copy in self.first(c, axis):
-                    copy.wait_recv()
+                wait_for(self.refs[axis].at[c, 0, far], self.sems[1].at[c, axis, 0])
                 for copy in self.second(c, axis):
                     copy.start()
 
         def end(self, c, absolute):
             for axis in range(2):
-                for copy in self.near(c, axis) + self.second(c, axis):
-                    copy.wait_recv()
+                wait_for(self.refs[axis].at[c, far, far], self.sems[1].at[c, axis, 1])
+                wait_for(self.refs[axis].at[c, far, 0], self.sems[1].at[c, axis, 2])
             rows = [[], []]
             for axis in range(2):
                 blocks = []
@@ -338,8 +336,9 @@
 
         def drain(self, c):
             for axis in range(2):
-                for copy in self.first(c, axis) + self.near(c, axis) + self.second(c, axis):
-                    copy.wait_send()
+                wait_for(self.refs[axis].at[c, 0, far], self.sems[0].at[c, axis, 0])
+                wait_for(self.refs[axis].at[c, far, far], self.sems[0].at[c, axis, 1])
+                wait_for(self.refs[axis].at[c, far, 0], self.sems[0].at[c, axis, 2])
 
     def unfold(left, right):
         return jnp.concatenate([left[0:ROWS], right[0:ROWS], left[ROWS:], right[ROWS:]], axis=1)
@@ -349,11 +348,19 @@
     sum2 = Sum((send2a, send2b), (early2a, early2b), (middle2a, middle2b), (late2a, late2b), (ss1, rs1))
     spread2 = Gather((gather2a, gather2b), (ss2, rs2))
 
-    for c in range(CHUNKS):
-        part = slice(c * PART, (c + 1) * PART)
-        square = dot(squares2[:, part], pick_one, TN)
+    loads[2].wait()
+    shared[0].wait()
+    for c in range(CHUNKS):
+        own_lanes = pl.ds(pl.multiple_of(core * MINE + c * PART, PART), PART)
+        mine = gained_own[:, own_lanes]
+        gained_swaps[c].wait()
+        theirs = gained_recv[c]
+        lower = jnp.where(core == 0, mine[0:HALF], theirs[0:HALF])
+        upper = jnp.where(core == 0, theirs[0:HALF], mine[0:HALF])
+        channels = jnp.concatenate([lower, upper], axis=0)
+        squares2 = jnp.concatenate([mine[HALF:], theirs[HALF:]], axis=0)
+        square = dot(squares2, pick_one, TN)
         square = folded(square, square)
-        channels = both[:, part]
         for axis in range(2):
             low_at = slice(axis * LANES, (axis + 1) * LANES)
             high_at = slice(FOLD + axis * LANES, FOLD + (axis + 1) * LANES)
@@ -486,7 +493,7 @@
         normed = spread2.end(c, True)
         theirs_next = dot(wn[1 - core].reshape(3 * HALF, WIDTH), normed, NT)
         next_send[c] = theirs_next.astype(BF16).reshape(3, HALF, PART)
-        swaps.append(to_sibling(next_send.at[c], next_recv.at[c], 7 + c))
+        swaps.append(to_sibling(next_send.at[c], next_recv.at[c], 6 + CHUNKS + c))
         swaps[c].start()
         own_next = dot(wn[core].reshape(3 * HALF, WIDTH), normed, NT)
         here = pl.ds(pl.multiple_of(core * MINE + c * PART, PART), PART)
@@ -572,8 +579,8 @@
             pltpu.VMEM((HALF, TOKENS), BF16),
             pltpu.VMEM((REQUESTS, KEYS), F32),
             pltpu.VMEM((HALF + STEPS, TOKENS), BF16),
-            pltpu.VMEM((HALF + STEPS, MINE), BF16),
-            pltpu.VMEM((HALF + STEPS, MINE), BF16),
+            pltpu.VMEM((CHUNKS, HALF + STEPS, PART), BF16),
+            pltpu.VMEM((CHUNKS, HALF + STEPS, PART), BF16),
             *sum_buffers(LANES + EXTRA), *gather_buffers(),
             pltpu.VMEM((CHUNKS, ROWS, WIDTH), F32),
             *sum_buffers(LANES), *gather_buffers(),
@@ -583,8 +590,8 @@
             pltpu.VMEM((EDGES, REQUESTS, HALF), BF16),
             pltpu.VMEM((GROUPS, REQUESTS, HALF, KEYS), BF16),
             pltpu.VMEM((GROUPS, EDGES, REQUESTS, HALF), BF16),
-            dma((9 + CHUNKS,)), dma((8,)), dma((7 + CHUNKS,)), dma((7 + CHUNKS,)),
-            *[dma((CHUNKS, 2, 3, SIDE - 1))] * 4,
+            dma((9 + CHUNKS,)), dma((8,)), dma((6 + 2 * CHUNKS,)), dma((6 + 2 * CHUNKS,)),
+            *[dma((CHUNKS, 2, 3))] * 4,
             dma((2, GROUPS - 1)), dma((2, GROUPS - 1)),
         ],
         compiler_params=pltpu.CompilerParams(

time: 61.8 us -> 60.8 us (0.984)
  Pallas kernels: 61 us -> 60.1 us
    pallas_call x1, Pallas kernels: 58.9 us -> 58 us  [per_device(): pl.pallas_call(kernel, name='draft_check', out_shape=outputs, in_specs=[a...]
where the time goes in v7:
time: 60.8 us; the launch traced here: 60.7 us
  Pallas kernels  60.1 us (99%)
  between operations  0.65 us (1%)
    pallas_call x1, Pallas kernels, per_device(): pl.pallas_call(kernel, name='draft_check', out_shape=outputs, in_specs=[a...  58 us
    pallas_call x1, Pallas kernels, per_device(): pl.pallas_call(finish, name='finish', out_shape=outputs, in_specs=[anywhe...  2.08 us

profile of v7, /device:TPU:1, one launch (start us, length us, event | category | flops | bytes accessed | tf_op | source)
XLA Modules:
  0.0 60.7 jit_solution(12914010576154429601)
XLA Ops:
  0.6 58.0 %draft_check.1 = (bf16[3,64,512]{2,1,0:T(8,128)(2,1)}, f32[32,64,128]{2,1,0:T(8,128)}, bf16[3,32,64]{2,1,0:T(8,128)(2,1)}) custom-call(bf16[512,2048]{1,0:T(8,128)(2,1)} %residual.1, bf16[3,64,512]{2,1,0:T(8,128)(2,1)} %bitcast.16, f32[16,128]{1,0:T(8,128)} %bitcast.18, f32[4,64]{1,0:T(4,128)} %taps_in.1, bf16[3,32,64]{2,1,0:T(8,128)(2,1)} %bitcast.17, ...), custom_call_target="tpu_custom_call" | custom-call | tf_op jit(solution)/shard_map/draft_check/pallas_call | solution.py:552
  58.6 2.1 %finish.1 = (bf16[3,64,512]{2,1,0:T(8,128)(2,1)}, f32[32,64,128]{2,1,0:T(8,128)}, bf16[3,32,64]{2,1,0:T(8,128)(2,1)}) custom-call(bf16[3,64,512]{2,1,0:T(8,128)(2,1)} %get-tuple-element.9.next_in, f32[32,64,128]{2,1,0:T(8,128)} %get-tuple-element.10.kept_in, bf16[3,32,64]{2,1,0:T(8,128)(2,1)} %get-tuple-element.11.edge_in), custom_call_target="tpu_custom_call" | custom-call | tf_op jit(solution)/shard_map/finish/pallas_call | solution.py:617

commit v8 on v7

--- a/solution.py
+++ b/solution.py
@@ -227,26 +227,30 @@
 
 
     class Sum:
-        def __init__(self, sends, early, middle, late, sems):
+        def __init__(self, sends, early, middle, late, sems, squares):
             self.sends, self.early, self.middle, self.late, self.sems = sends, early, middle, late, sems
+            self.squares = squares
+
+        def lanes(self, c, axis):
+            return slice(0, LANES + EXTRA if self.squares and axis == c % 2 else LANES)
 
         def first(self, c, axis):
             return [
-                link(self.sends[axis].at[c, k, far], self.early[axis].at[c, k, far],
+                link(self.sends[axis].at[c, k, far, :, self.lanes(c, axis)], self.early[axis].at[c, k, far, :, self.lanes(c, axis)],
                      *self.sems, c, axis, 0, k, axis)
                 for k in range(1, SIDE)
             ]
 
         def near(self, c, axis):
             return [
-                link(self.sends[axis].at[c, k, 0], self.early[axis].at[c, k, 0],
+                link(self.sends[axis].at[c, k, 0, :, self.lanes(c, axis)], self.early[axis].at[c, k, 0, :, self.lanes(c, axis)],
                      *self.sems, c, axis, 2, k, axis)
                 for k in range(1, SIDE)
             ]
 
         def second(self, c, axis):
             return [
-                link(self.middle[axis].at[c, k], self.late[axis].at[c, k],
+                link(self.middle[axis].at[c, k, :, self.lanes(c, axis)], self.late[axis].at[c, k, :, self.lanes(c, axis)],
                      *self.sems, c, axis, 1, k, 1 - axis)
                 for k in range(1, SIDE)
             ]
@@ -256,27 +260,27 @@
                 copy.start()
 
         def turn(self, c, axis):
-            wait_for(self.early[axis].at[c, far, far], self.sems[1].at[c, axis, 0])
-            sums = self.sends[axis][c, 0, far].astype(F32)
+            wait_for(self.early[axis].at[c, far, far, :, self.lanes(c, axis)], self.sems[1].at[c, axis, 0])
+            sums = self.sends[axis][c, 0, far, :, self.lanes(c, axis)].astype(F32)
             for k in range(1, SIDE):
-                sums = sums + self.early[axis][c, k, far].astype(F32)
-            self.middle[axis][c, far] = sums.astype(BF16)
+                sums = sums + self.early[axis][c, k, far, :, self.lanes(c, axis)].astype(F32)
+            self.middle[axis][c, far, :, self.lanes(c, axis)] = sums.astype(BF16)
             for copy in self.second(c, axis) + self.near(c, axis):
                 copy.start()
 
         def end(self, c, axis):
-            wait_for(self.late[axis].at[c, far], self.sems[1].at[c, axis, 1])
-            wait_for(self.early[axis].at[c, far, 0], self.sems[1].at[c, axis, 2])
-            sums = self.sends[axis][c, 0, 0].astype(F32)
+            wait_for(self.late[axis].at[c, far, :, self.lanes(c, axis)], self.sems[1].at[c, axis, 1])
+            wait_for(self.early[axis].at[c, far, 0, :, self.lanes(c, axis)], self.sems[1].at[c, axis, 2])
+            sums = self.sends[axis][c, 0, 0, :, self.lanes(c, axis)].astype(F32)
             for k in range(1, SIDE):
-                sums = sums + self.early[axis][c, k, 0].astype(F32)
-                sums = sums + self.late[axis][c, k].astype(F32)
+                sums = sums + self.early[axis][c, k, 0, :, self.lanes(c, axis)].astype(F32)
+                sums = sums + self.late[axis][c, k, :, self.lanes(c, axis)].astype(F32)
             return sums
 
         def drain(self, c, axis):
-            wait_for(self.sends[axis].at[c, far, far], self.sems[0].at[c, axis, 0])
-            wait_for(self.middle[axis].at[c, far], self.sems[0].at[c, axis, 1])
-            wait_for(self.sends[axis].at[c, far, 0], self.sems[0].at[c, axis, 2])
+            wait_for(self.sends[axis].at[c, far, far, :, self.lanes(c, axis)], self.sems[0].at[c, axis, 0])
+            wait_for(self.middle[axis].at[c, far, :, self.lanes(c, axis)], self.sems[0].at[c, axis, 1])
+            wait_for(self.sends[axis].at[c, far, 0, :, self.lanes(c, axis)], self.sems[0].at[c, axis, 2])
 
     class Gather:
         def __init__(self, refs, sems):
@@ -343,9 +347,9 @@
     def unfold(left, right):
         return jnp.concatenate([left[0:ROWS], right[0:ROWS], left[ROWS:], right[ROWS:]], axis=1)
 
-    sum1 = Sum((send1a, send1b), (early1a, early1b), (middle1a, middle1b), (late1a, late1b), (ss1, rs1))
+    sum1 = Sum((send1a, send1b), (early1a, early1b), (middle1a, middle1b), (late1a, late1b), (ss1, rs1), True)
     spread1 = Gather((gather1a, gather1b), (ss2, rs2))
-    sum2 = Sum((send2a, send2b), (early2a, early2b), (middle2a, middle2b), (late2a, late2b), (ss1, rs1))
+    sum2 = Sum((send2a, send2b), (early2a, early2b), (middle2a, middle2b), (late2a, late2b), (ss1, rs1), False)
     spread2 = Gather((gather2a, gather2b), (ss2, rs2))
 
     loads[2].wait()
@@ -357,7 +361,7 @@
         theirs = gained_recv[c]
         lower = jnp.where(core == 0, mine[0:HALF], theirs[0:HALF])
         upper = jnp.where(core == 0, theirs[0:HALF], mine[0:HALF])
-        channels = jnp.concatenate([lower, upper], axis=0)
+        channels = jnp.concatenate([lower, upper], axis=0).T
         squares2 = jnp.concatenate([mine[HALF:], theirs[HALF:]], axis=0)
         square = dot(squares2, pick_one, TN)
         square = folded(square, square)
@@ -365,9 +369,9 @@
             low_at = slice(axis * LANES, (axis + 1) * LANES)
             high_at = slice(FOLD + axis * LANES, FOLD + (axis + 1) * LANES)
             terms = folded(
-                dot(channels, wo[:, :, low_at].reshape(2 * HALF, LANES), TN),
-                dot(channels, wo[:, :, high_at].reshape(2 * HALF, LANES), TN))
-            if axis == 0:
+                dot(channels, wo[:, :, low_at].reshape(2 * HALF, LANES)),
+                dot(channels, wo[:, :, high_at].reshape(2 * HALF, LANES)))
+            if axis == c % 2:
                 terms = jnp.concatenate([terms, square], axis=2)
             put(terms, sum1.sends[axis], c, axis, True)
             sum1.begin(c, axis)
@@ -430,8 +434,8 @@
         right = sum1.end(c, 1)
         near = res_v[c].astype(F32)
         before = jnp.where(chip % 2 == 0, near[0:ROWS], near[ROWS:])
-        square = left[0:ROWS, LANES:LANES + 1]
-        attn = unfold(left[:, 0:LANES], right) * lax.rsqrt(square / WIDTH + EPSILON)
+        square = (left if c % 2 == 0 else right)[0:ROWS, LANES:LANES + 1]
+        attn = unfold(left[:, 0:LANES], right[:, 0:LANES]) * lax.rsqrt(square / WIDTH + EPSILON)
         first = (before + attn).astype(BF16).astype(F32)
         first_v[c] = first
         spread1.begin(c, scaled_norm(first, gain_mlp[...]))
@@ -445,15 +449,16 @@
 
     hidden_width = wd.shape[0] * wd.shape[1]
     for c in range(CHUNKS):
-        both_parts = dot(wgu[...].reshape(2 * hidden_width, WIDTH), spread1.end(c, False), NT)
-        gate = both_parts[0:hidden_width]
-        hidden = (gate * jax.nn.sigmoid(gate) * both_parts[hidden_width:]).astype(BF16)
+        rows = spread1.end(c, False)
+        both_parts = dot(rows, wgu[...].reshape(2 * hidden_width, WIDTH), NT)
+        gate = both_parts[:, 0:hidden_width]
+        hidden = (gate * jax.nn.sigmoid(gate) * both_parts[:, hidden_width:]).astype(BF16)
         for axis in range(2):
             low_at = slice(axis * LANES, (axis + 1) * LANES)
             high_at = slice(FOLD + axis * LANES, FOLD + (axis + 1) * LANES)
             put(folded(
-                dot(hidden, wd[:, :, low_at].reshape(hidden_width, LANES), TN),
-                dot(hidden, wd[:, :, high_at].reshape(hidden_width, LANES), TN),
+                dot(hidden, wd[:, :, low_at].reshape(hidden_width, LANES)),
+                dot(hidden, wd[:, :, high_at].reshape(hidden_width, LANES)),
             ), sum2.sends[axis], c, axis, False)
             sum2.begin(c, axis)
     for c in range(CHUNKS):
@@ -525,11 +530,9 @@
         copy.wait()
 
 
-def sum_buffers(width_a):
+def sum_buffers(width):
     grids = [(SIDE, SIDE), (SIDE, SIDE), (SIDE,), (SIDE,)]
-    return [
-        pltpu.VMEM((CHUNKS, *grid, 2 * ROWS, width), BF16) for grid in grids for width in (width_a, LANES)
-    ]
+    return [pltpu.VMEM((CHUNKS, *grid, 2 * ROWS, width), BF16) for grid in grids for _ in range(2)]
 
 
 def gather_buffers():

time: 60.8 us -> 59.5 us (0.979)
  Pallas kernels: 60.1 us -> 58.7 us
    pallas_call x1, Pallas kernels: 58 us -> 56.6 us  [per_device(): pl.pallas_call(kernel, name='draft_check', out_shape=outputs, in_specs=[a...]
where the time goes in v8:
time: 59.5 us; the launch traced here: 59.4 us
  Pallas kernels  58.7 us (99%)
  between operations  0.65 us (1%)
    pallas_call x1, Pallas kernels, per_device(): pl.pallas_call(kernel, name='draft_check', out_shape=outputs, in_specs=[a...  56.6 us
    pallas_call x1, Pallas kernels, per_device(): pl.pallas_call(finish, name='finish', out_shape=outputs, in_specs=[anywhe...  2.08 us

profile of v8, /device:TPU:1, one launch (start us, length us, event | category | flops | bytes accessed | tf_op | source)
XLA Modules:
  0.0 59.4 jit_solution(7735323486283650016)
XLA Ops:
  0.6 56.6 %draft_check.1 = (bf16[3,64,512]{2,1,0:T(8,128)(2,1)}, f32[32,64,128]{2,1,0:T(8,128)}, bf16[3,32,64]{2,1,0:T(8,128)(2,1)}) custom-call(bf16[512,2048]{1,0:T(8,128)(2,1)} %residual.1, bf16[3,64,512]{2,1,0:T(8,128)(2,1)} %bitcast.16, f32[16,128]{1,0:T(8,128)} %bitcast.18, f32[4,64]{1,0:T(4,128)} %taps_in.1, bf16[3,32,64]{2,1,0:T(8,128)(2,1)} %bitcast.17, ...), custom_call_target="tpu_custom_call" | custom-call | tf_op jit(solution)/shard_map/draft_check/pallas_call | solution.py:555
  57.3 2.1 %finish.1 = (bf16[3,64,512]{2,1,0:T(8,128)(2,1)}, f32[32,64,128]{2,1,0:T(8,128)}, bf16[3,32,64]{2,1,0:T(8,128)(2,1)}) custom-call(bf16[3,64,512]{2,1,0:T(8,128)(2,1)} %get-tuple-element.9.next_in, f32[32,64,128]{2,1,0:T(8,128)} %get-tuple-element.10.kept_in, bf16[3,32,64]{2,1,0:T(8,128)(2,1)} %get-tuple-element.11.edge_in), custom_call_target="tpu_custom_call" | custom-call | tf_op jit(solution)/shard_map/finish/pallas_call | solution.py:620

commit v9 on v8

--- a/solution.py
+++ b/solution.py
@@ -221,6 +221,7 @@
             recv_sem=rsem.at[c, axis, stage], device_id=along(towards, k), device_id_type=MESH)
 
     far = slice(1, SIDE)
+    opposite_first = (2, 1, 3)
 
     def wait_for(region, sem):
         pltpu.make_async_copy(region, region, sem).wait()
@@ -238,21 +239,21 @@
             return [
                 link(self.sends[axis].at[c, k, far, :, self.lanes(c, axis)], self.early[axis].at[c, k, far, :, self.lanes(c, axis)],
                      *self.sems, c, axis, 0, k, axis)
-                for k in range(1, SIDE)
+                for k in opposite_first
             ]
 
         def near(self, c, axis):
             return [
                 link(self.sends[axis].at[c, k, 0, :, self.lanes(c, axis)], self.early[axis].at[c, k, 0, :, self.lanes(c, axis)],
                      *self.sems, c, axis, 2, k, axis)
-                for k in range(1, SIDE)
+                for k in opposite_first
             ]
 
         def second(self, c, axis):
             return [
                 link(self.middle[axis].at[c, k, :, self.lanes(c, axis)], self.late[axis].at[c, k, :, self.lanes(c, axis)],
                      *self.sems, c, axis, 1, k, 1 - axis)
-                for k in range(1, SIDE)
+                for k in opposite_first
             ]
 
         def begin(self, c, axis):
@@ -290,21 +291,21 @@
             ref = self.refs[axis]
             return [
                 link(ref.at[c, 0, 0], ref.at[c, 0, SIDE - k], *self.sems, c, axis, 0, k, 1 - axis)
-                for k in range(1, SIDE)
+                for k in opposite_first
             ]
 
         def near(self, c, axis):
             ref = self.refs[axis]
             return [
                 link(ref.at[c, 0, 0], ref.at[c, SIDE - k, 0], *self.sems, c, axis, 2, k, axis)
-                for k in range(1, SIDE)
+                for k in opposite_first
             ]
 
         def second(self, c, axis):
             ref = self.refs[axis]
             return [
                 link(ref.at[c, 0, far], ref.at[c, SIDE - k, far], *self.sems, c, axis, 1, k, axis)
-                for k in range(1, SIDE)
+                for k in opposite_first
             ]
 
         def begin(self, c, rows):

time: 59.5 us -> 58.3 us (0.980)
  Pallas kernels: 58.7 us -> 57.5 us
    pallas_call x1, Pallas kernels: 56.6 us -> 55.5 us  [per_device(): pl.pallas_call(kernel, name='draft_check', out_shape=outputs, in_specs=[a...]
where the time goes in v9:
time: 58.3 us; the launch traced here: 58.2 us
  Pallas kernels  57.5 us (99%)
  between operations  0.65 us (1%)
    pallas_call x1, Pallas kernels, per_device(): pl.pallas_call(kernel, name='draft_check', out_shape=outputs, in_specs=[a...  55.5 us
    pallas_call x1, Pallas kernels, per_device(): pl.pallas_call(finish, name='finish', out_shape=outputs, in_specs=[anywhe...  2.08 us

profile of v9, /device:TPU:1, one launch (start us, length us, event | category | flops | bytes accessed | tf_op | source)
XLA Modules:
  0.0 58.2 jit_solution(5783211300860316609)
XLA Ops:
  0.6 55.5 %draft_check.1 = (bf16[3,64,512]{2,1,0:T(8,128)(2,1)}, f32[32,64,128]{2,1,0:T(8,128)}, bf16[3,32,64]{2,1,0:T(8,128)(2,1)}) custom-call(bf16[512,2048]{1,0:T(8,128)(2,1)} %residual.1, bf16[3,64,512]{2,1,0:T(8,128)(2,1)} %bitcast.16, f32[16,128]{1,0:T(8,128)} %bitcast.18, f32[4,64]{1,0:T(4,128)} %taps_in.1, bf16[3,32,64]{2,1,0:T(8,128)(2,1)} %bitcast.17, ...), custom_call_target="tpu_custom_call" | custom-call | tf_op jit(solution)/shard_map/draft_check/pallas_call | solution.py:556
  56.1 2.1 %finish.1 = (bf16[3,64,512]{2,1,0:T(8,128)(2,1)}, f32[32,64,128]{2,1,0:T(8,128)}, bf16[3,32,64]{2,1,0:T(8,128)(2,1)}) custom-call(bf16[3,64,512]{2,1,0:T(8,128)(2,1)} %get-tuple-element.9.next_in, f32[32,64,128]{2,1,0:T(8,128)} %get-tuple-element.10.kept_in, bf16[3,32,64]{2,1,0:T(8,128)(2,1)} %get-tuple-element.11.edge_in), custom_call_target="tpu_custom_call" | custom-call | tf_op jit(solution)/shard_map/finish/pallas_call | solution.py:621

commit v10 on v9

--- a/solution.py
+++ b/solution.py
@@ -481,7 +481,7 @@
     source_lane = iota((1, GROUPS * REQUESTS), 1)
     for i in range(REQUESTS):
         found = jnp.max(jnp.where(home_row == group * REQUESTS + i, source_lane, 0))
-        kept_out[i] = kept_all[found // REQUESTS, found % REQUESTS].astype(F32)
+        kept_out[i] = kept_all[found // REQUESTS, found % REQUESTS]
     leaving = pltpu.make_async_copy(kept_out, kept_home, load_sem.at[8 + CHUNKS])
     leaving.start()
     target_row = iota((REQUESTS, GROUPS * REQUESTS), 0) + group * REQUESTS
@@ -516,16 +516,18 @@
 PIECE = REQUESTS // PIECES
 
 
-def finish(next_in, kept_in, edge_in, next_out, kept_out, edge_out, next_v, kept_v, edge_v, in_sems, out_sems):
+def finish(next_in, kept_in, edge_in, next_out, kept_out, edge_out, next_v, kept_v, edge_v, narrow_v, in_sems, out_sems):
     parts = [slice(i * PIECE, (i + 1) * PIECE) for i in range(PIECES)]
-    routes = [(kept_in.at[part], kept_v.at[part], kept_out.at[part]) for part in parts]
-    routes += [(next_in, next_v, next_out), (edge_in, edge_v, edge_out)]
-    arrive = [pltpu.make_async_copy(a, b, in_sems.at[i]) for i, (a, b, _) in enumerate(routes)]
-    leave = [pltpu.make_async_copy(b, c, out_sems.at[i]) for i, (_, b, c) in enumerate(routes)]
+    routes = [(kept_in.at[part], narrow_v.at[part], kept_v.at[part], kept_out.at[part]) for part in parts]
+    routes += [(next_in, next_v, next_v, next_out), (edge_in, edge_v, edge_v, edge_out)]
+    arrive = [pltpu.make_async_copy(a, b, in_sems.at[i]) for i, (a, b, _, _) in enumerate(routes)]
+    leave = [pltpu.make_async_copy(b, c, out_sems.at[i]) for i, (_, _, b, c) in enumerate(routes)]
     for copy in arrive:
         copy.start()
-    for copy, further in zip(arrive, leave):
+    for i, (copy, further) in enumerate(zip(arrive, leave)):
         copy.wait()
+        if i < PIECES:
+            kept_v[parts[i]] = narrow_v[parts[i]].astype(F32)
         further.start()
     for copy in leave:
         copy.wait()
@@ -556,7 +558,7 @@
     results = pl.pallas_call(
         kernel,
         name="draft_check",
-        out_shape=outputs,
+        out_shape=(outputs[0], jax.ShapeDtypeStruct(outputs[1].shape, BF16), outputs[2]),
         in_specs=[anywhere] * 16,
         out_specs=(vmem, anywhere, vmem),
         scratch_shapes=[
@@ -568,7 +570,7 @@
             pltpu.VMEM((1, HALF), F32),
             pltpu.VMEM((1, WIDTH), F32),
             pltpu.VMEM((1, WIDTH), F32),
-            pltpu.VMEM((REQUESTS, HALF, KEYS), F32),
+            pltpu.VMEM((REQUESTS, HALF, KEYS), BF16),
             pltpu.VMEM((3, HALF, TOKENS), BF16),
             pltpu.VMEM((2, 2, HALF, TOKENS), BF16),
             pltpu.VMEM((REQUESTS, HALF, KEYS), F32),
@@ -626,6 +628,7 @@
         out_specs=(anywhere,) * 3,
         scratch_shapes=[
             *[pltpu.VMEM(output.shape, output.dtype) for output in outputs],
+            pltpu.VMEM(outputs[1].shape, BF16),
             dma((PIECES + 2,)), dma((PIECES + 2,)),
         ],
         compiler_params=pltpu.CompilerParams(vmem_limit_bytes=56 * 2**20),

time: 58.3 us -> 58.3 us (level)
  no operation moved by 1% of the time
where the time goes in v10:
time: 58.3 us; the launch traced here: 58.1 us
  Pallas kernels  57.5 us (99%)
  between operations  0.65 us (1%)
    pallas_call x1, Pallas kernels, per_device(): pl.pallas_call(kernel, name='draft_check', out_shape=(outputs[0], jax.Sha...  55.4 us
    pallas_call x1, Pallas kernels, per_device(): pl.pallas_call(finish, name='finish', out_shape=outputs, in_specs=[anywhe...  2.05 us

profile of v10, /device:TPU:1, one launch (start us, length us, event | category | flops | bytes accessed | tf_op | source)
XLA Modules:
  0.0 58.1 jit_solution(14436659537350780343)
XLA Ops:
  0.6 55.4 %draft_check.1 = (bf16[3,64,512]{2,1,0:T(8,128)(2,1)}, bf16[32,64,128]{2,1,0:T(8,128)(2,1)}, bf16[3,32,64]{2,1,0:T(8,128)(2,1)}) custom-call(bf16[512,2048]{1,0:T(8,128)(2,1)} %residual.1, bf16[3,64,512]{2,1,0:T(8,128)(2,1)} %bitcast.16, f32[16,128]{1,0:T(8,128)} %bitcast.18, f32[4,64]{1,0:T(4,128)} %taps_in.1, bf16[3,32,64]{2,1,0:T(8,128)(2,1)} %bitcast.17, ...), custom_call_target="tpu_custom_call" | custom-call | tf_op jit(solution)/shard_map/draft_check/pallas_call | solution.py:558
  56.1 2.1 %finish.1 = (bf16[3,64,512]{2,1,0:T(8,128)(2,1)}, f32[32,64,128]{2,1,0:T(8,128)}, bf16[3,32,64]{2,1,0:T(8,128)(2,1)}) custom-call(bf16[3,64,512]{2,1,0:T(8,128)(2,1)} %get-tuple-element.9.next_in, bf16[32,64,128]{2,1,0:T(8,128)(2,1)} %get-tuple-element.10.kept_in, bf16[3,32,64]{2,1,0:T(8,128)(2,1)} %get-tuple-element.11.edge_in), custom_call_target="tpu_custom_call" | custom-call | tf_op jit(solution)/shard_map/finish/pallas_call | solution.py:623
